TPU v7x, 32 devices: a whole 2x2x4 slice. The times are simulated.
32 devices in a mesh: batch: 8 (over y, x, core), row: 4 (over z).
Axes of the slice: x: 2, y: 2, z: 4, core: 2. Of those that a mesh axis runs over, the one named last changes fastest.
Arguments:
- images: bfloat16 [2, 64, 128, 1536], P(None, 'batch', 'row'), may hold values from -6 to 6
- bucket: int32 [2, 64], P(None, 'batch'), may hold values 0 or 1
- cotangent: bfloat16 [2, 64, 128, 1536], P(None, 'batch', 'row'), may hold values from -6 to 6
- narrow_kernel: bfloat16 [768, 1536], P(('batch', 'row')), may hold values from -0.15625 to 0.15625
- narrow_gain: bfloat16 [768], P(('batch', 'row')), may hold values from 0.25 to 1.75
- narrow_bias: bfloat16 [768], P(('batch', 'row')), may hold values from -3 to 3
- first_kernel: bfloat16 [768, 1152], P(('batch', 'row')), may hold values from -0.1875 to 0.1875
- first_gain: bfloat16 [768], P(('batch', 'row')), may hold values from 0.25 to 1.75
- first_bias: bfloat16 [768], P(('batch', 'row')), may hold values from -3 to 3
- second_kernel: bfloat16 [768, 1152], P(('batch', 'row')), may hold values from -0.1875 to 0.1875
- second_gain: bfloat16 [768], P(('batch', 'row')), may hold values from 0.25 to 1.75
- second_bias: bfloat16 [768], P(('batch', 'row')), may hold values from -3 to 3
- widen_kernel: bfloat16 [1536, 768], P(('batch', 'row')), may hold values from -0.21875 to 0.21875
- widen_gain: bfloat16 [1536], P(('batch', 'row')), may hold values from 0.25 to 1.75
- widen_bias: bfloat16 [1536], P(('batch', 'row')), may hold values from -3 to 3
- squeeze_kernel: bfloat16 [768, 1536], P(('batch', 'row')), may hold values from -0.625 to 0.625
- squeeze_bias: bfloat16 [768], P(('batch', 'row')), may hold values from -3 to 3
- excite_kernel: bfloat16 [1536, 768], P(('batch', 'row')), may hold values from -0.4375 to 0.4375
- excite_bias: bfloat16 [1536], P(('batch', 'row')), may hold values from -3 to 3
- skip_gain: bfloat16 [1], replicated, may hold values from 3 to 6
Outputs:
- output: bfloat16 [2, 64, 128, 1536], P(None, 'batch', 'row')
- input_grad: bfloat16 [2, 64, 128, 1536], P(None, 'batch', 'row')
- narrow_kernel_grad: float32 [768, 1536], P(('batch', 'row'))
- narrow_gain_grad: float32 [768], P(('batch', 'row'))
- narrow_bias_grad: float32 [768], P(('batch', 'row'))
- first_kernel_grad: float32 [768, 1152], P(('batch', 'row'))
- first_gain_grad: float32 [768], P(('batch', 'row'))
- first_bias_grad: float32 [768], P(('batch', 'row'))
- second_kernel_grad: float32 [768, 1152], P(('batch', 'row'))
- second_gain_grad: float32 [768], P(('batch', 'row'))
- second_bias_grad: float32 [768], P(('batch', 'row'))
- widen_kernel_grad: float32 [1536, 768], P(('batch', 'row'))
- widen_gain_grad: float32 [1536], P(('batch', 'row'))
- widen_bias_grad: float32 [1536], P(('batch', 'row'))
- squeeze_kernel_grad: float32 [768, 1536], P(('batch', 'row'))
- squeeze_bias_grad: float32 [768], P(('batch', 'row'))
- excite_kernel_grad: float32 [1536, 768], P(('batch', 'row'))
- excite_bias_grad: float32 [1536], P(('batch', 'row'))
- skip_gain_grad: float32 [1], replicated
All inputs are finite; a program needn't handle non-finite values. No bound on the sum of `bucket` on one device may be relied on, other than what follows from the above.
Results may differ from a plain program's by a relative error of at most 0.04.
Values may be sent and summed in bfloat16 or wider, within the bound.
A program may use at most 192 MiB of HBM per device.

v0:
```python
import jax
import jax.numpy as jnp
from jax import lax
from jax.sharding import PartitionSpec as P

GW = 128
PIX = 128


gamma_act = 1.7015
alpha_res = 0.2
beta_in = 0.9622504486493763
eps_std = 0.0001


def with_halo(block, sides, width):
    for axis, dim in sides:
        count = lax.axis_size(axis)
        forward = [(i, i + 1) for i in range(count - 1)]
        backward = [(target, source) for source, target in forward]
        low = lax.ppermute(
            lax.slice_in_dim(block, block.shape[dim] - width, None, axis=dim), axis, forward
        )
        high = lax.ppermute(lax.slice_in_dim(block, 0, width, axis=dim), axis, backward)
        block = jnp.concatenate([low, block, high], axis=dim)
    return block


def scaled_gelu(value):
    return gamma_act * jax.nn.gelu(value)


def input_act(value):
    return scaled_gelu(value) * beta_in


def double_sigmoid(value):
    return 2.0 * jax.nn.sigmoid(value)


def standard(kernel, gain):
    fan = kernel.shape[1]
    center = jnp.mean(kernel, axis=1, keepdims=True)
    spread_sq = jnp.mean(jnp.square(kernel - center), axis=1, keepdims=True)
    return gain[:, None] * (kernel - center) * lax.rsqrt(fan * spread_sq + eps_std)


def pull_back(func, value, cotan):
    return jax.vjp(func, value)[1](cotan)[0]


def columns(padded, wide, strip):
    blocks = padded.shape[0]
    groups = padded.shape[2] // GW
    places = jnp.arange(strip)
    pieces = []
    for step_row in (-1, 0, 1):
        for step_col in (-1, 0, 1):
            start_wide = 17 + step_row * 16 + step_col
            start_tall = 17 + step_row * 8 + step_col
            wide_part = lax.slice_in_dim(padded, start_wide, start_wide + strip, axis=1)
            tall_part = lax.slice_in_dim(padded, start_tall, start_tall + strip, axis=1)
            wide_ok = (places % 16 + step_col >= 0) & (places % 16 + step_col < 16)
            tall_ok = (places % 8 + step_col >= 0) & (places % 8 + step_col < 8)
            keep = jnp.where(wide[:, None], wide_ok[None, :], tall_ok[None, :])
            chosen = jnp.where(wide[:, None, None], wide_part, tall_part)
            chosen = jnp.where(keep[:, :, None], chosen, jnp.zeros_like(chosen))
            pieces.append(chosen.reshape(blocks, strip, groups, GW))
    stacked = jnp.stack(pieces, axis=3)
    return stacked.reshape(blocks * strip, groups, 9 * GW)


def forward_columns(field, wide):
    strip = field.shape[1]
    extended = with_halo(field, (("row", 1),), 16)
    return columns(jnp.pad(extended, ((0, 0), (1, 1), (0, 0))), wide, strip)


def backward_columns(field, wide):
    strip = field.shape[1]
    extended = with_halo(field, (("row", 1),), 16)
    return columns(jnp.pad(extended, ((0, 0), (1, 1), (0, 0))), wide, strip)


def spread(cols, kernel):
    groups = kernel.shape[0] // GW
    shaped = kernel.reshape(groups, GW, 9 * GW)
    result = jnp.einsum("rgk,gok->rgo", cols, shaped, preferred_element_type=jnp.float32)
    return result.reshape(cols.shape[0], groups * GW)


def flipped(kernel):
    groups = kernel.shape[0] // GW
    shaped = kernel.reshape(groups, GW, 9, GW)[:, :, ::-1, :]
    return jnp.transpose(shaped, (0, 3, 2, 1)).reshape(groups * GW, 9 * GW)


def kernel_grad(delta, cols):
    rows, groups, taps = cols.shape
    result = jnp.einsum(
        "rgo,rgk->gok", delta.reshape(rows, groups, GW), cols, preferred_element_type=jnp.float32
    )
    return result.reshape(groups * GW, taps)


def tuple_add(first, second):
    return tuple((left + right for left, right in zip(first, second)))


def micro_step(images_now, bucket_now, cotan_now, shared, skip, leader, count):
    (
        narrow_std,
        first_std,
        second_std,
        widen_std,
        squeeze_kernel,
        excite_kernel,
        narrow_bias,
        first_bias,
        second_bias,
        widen_bias,
        squeeze_bias,
        excite_bias,
    ) = shared
    blocks, strip, width = images_now.shape
    rows = blocks * strip
    wide = bucket_now == 0
    inputs = images_now.astype(jnp.float32)
    act_zero = input_act(inputs).astype(jnp.bfloat16).reshape(rows, width)
    pre_zero = jnp.einsum(
        "rd,md->rm", act_zero, narrow_std, preferred_element_type=jnp.float32
    ) + narrow_bias.astype(jnp.float32)
    act_one = scaled_gelu(pre_zero).astype(jnp.bfloat16).reshape(blocks, strip, -1)
    cols_one = forward_columns(act_one, wide)
    pre_one = spread(cols_one, first_std) + first_bias.astype(jnp.float32)
    act_two = scaled_gelu(pre_one).astype(jnp.bfloat16).reshape(blocks, strip, -1)
    cols_two = forward_columns(act_two, wide)
    pre_two = spread(cols_two, second_std) + second_bias.astype(jnp.float32)
    act_three = scaled_gelu(pre_two).astype(jnp.bfloat16)
    branch = jnp.einsum(
        "rm,dm->rd", act_three, widen_std, preferred_element_type=jnp.float32
    ) + widen_bias.astype(jnp.float32)
    branch_maps = branch.reshape(blocks, strip, width)
    pooled = (
        lax.psum(jnp.sum(branch_maps, axis=1).astype(jnp.bfloat16), "row").astype(jnp.float32) / PIX
    )
    pooled_low = pooled.astype(jnp.bfloat16)
    squeezed = jnp.einsum(
        "bd,md->bm", pooled_low, squeeze_kernel, preferred_element_type=jnp.float32
    ) + squeeze_bias.astype(jnp.float32)
    hidden_low = jax.nn.gelu(squeezed).astype(jnp.bfloat16)
    excited = jnp.einsum(
        "bm,dm->bd", hidden_low, excite_kernel, preferred_element_type=jnp.float32
    ) + excite_bias.astype(jnp.float32)
    gate = double_sigmoid(excited)
    output = (inputs + alpha_res * skip * (gate[:, None, :] * branch_maps)).astype(jnp.bfloat16)
    upstream = cotan_now.astype(jnp.float32)
    scaled = alpha_res * skip * upstream
    gate_grad = lax.psum(jnp.sum(scaled * branch_maps, axis=1).astype(jnp.bfloat16), "row").astype(
        jnp.float32
    )
    skip_part = jnp.sum(alpha_res * upstream * (gate[:, None, :] * branch_maps))
    excited_grad = pull_back(double_sigmoid, excited, gate_grad)
    excited_low = excited_grad.astype(jnp.bfloat16)
    excite_grad = jnp.einsum(
        "bd,bm->dm", excited_low, hidden_low, preferred_element_type=jnp.float32
    )
    hidden_grad = jnp.einsum(
        "bd,dm->bm", excited_low, excite_kernel, preferred_element_type=jnp.float32
    )
    squeezed_grad = pull_back(jax.nn.gelu, squeezed, hidden_grad)
    squeezed_low = squeezed_grad.astype(jnp.bfloat16)
    squeeze_grad = jnp.einsum(
        "bm,bd->md", squeezed_low, pooled_low, preferred_element_type=jnp.float32
    )
    pooled_grad = jnp.einsum(
        "bm,md->bd", squeezed_low, squeeze_kernel, preferred_element_type=jnp.float32
    )
    branch_grad = (scaled * gate[:, None, :] + pooled_grad[:, None, :] / PIX).reshape(rows, width)
    branch_low = branch_grad.astype(jnp.bfloat16)
    widen_grad = jnp.einsum("rd,rm->dm", branch_low, act_three, preferred_element_type=jnp.float32)
    three_grad = jnp.einsum("rd,dm->rm", branch_low, widen_std, preferred_element_type=jnp.float32)
    pre_two_grad = pull_back(scaled_gelu, pre_two, three_grad)
    two_low = pre_two_grad.astype(jnp.bfloat16)
    second_grad = kernel_grad(two_low, cols_two)
    two_grad = spread(
        backward_columns(two_low.reshape(blocks, strip, -1), wide), flipped(second_std)
    )
    pre_one_grad = pull_back(scaled_gelu, pre_one, two_grad)
    one_low = pre_one_grad.astype(jnp.bfloat16)
    first_grad = kernel_grad(one_low, cols_one)
    one_grad = spread(
        backward_columns(one_low.reshape(blocks, strip, -1), wide), flipped(first_std)
    )
    pre_zero_grad = pull_back(scaled_gelu, pre_zero, one_grad)
    zero_low = pre_zero_grad.astype(jnp.bfloat16)
    narrow_grad = jnp.einsum("rm,rd->md", zero_low, act_zero, preferred_element_type=jnp.float32)
    zero_grad = jnp.einsum("rm,md->rd", zero_low, narrow_std, preferred_element_type=jnp.float32)
    input_grad = (
        upstream + pull_back(input_act, inputs, zero_grad.reshape(blocks, strip, width))
    ).astype(jnp.bfloat16)
    grads = (
        narrow_grad,
        first_grad,
        second_grad,
        widen_grad,
        squeeze_grad * leader,
        excite_grad * leader,
        jnp.sum(pre_zero_grad, axis=0),
        jnp.sum(pre_one_grad, axis=0),
        jnp.sum(pre_two_grad, axis=0),
        jnp.sum(branch_grad, axis=0),
        jnp.sum(squeezed_grad, axis=0) * leader,
        jnp.sum(excited_grad, axis=0) * leader,
        jnp.full((count,), skip_part, jnp.float32),
    )
    return (output, input_grad, grads)


def body(
    images,
    bucket,
    cotangent,
    narrow_kernel,
    narrow_gain,
    narrow_bias,
    first_kernel,
    first_gain,
    first_bias,
    second_kernel,
    second_gain,
    second_bias,
    widen_kernel,
    widen_gain,
    widen_bias,
    squeeze_kernel,
    squeeze_bias,
    excite_kernel,
    excite_bias,
    skip_gain,
):
    count = lax.axis_size(("batch", "row"))
    leader = (lax.axis_index("row") == 0).astype(jnp.float32)
    skip = skip_gain.astype(jnp.float32)[0]
    narrow_std = standard(
        narrow_kernel.astype(jnp.float32), narrow_gain.astype(jnp.float32)
    ).astype(jnp.bfloat16)
    first_std = standard(first_kernel.astype(jnp.float32), first_gain.astype(jnp.float32)).astype(
        jnp.bfloat16
    )
    second_std = standard(
        second_kernel.astype(jnp.float32), second_gain.astype(jnp.float32)
    ).astype(jnp.bfloat16)
    widen_std = standard(widen_kernel.astype(jnp.float32), widen_gain.astype(jnp.float32)).astype(
        jnp.bfloat16
    )
    outputs = []
    input_grads = []
    summed = None
    for number in range(images.shape[0]):
        shared = (
            lax.all_gather(narrow_std, ("batch", "row"), axis=0, tiled=True),
            lax.all_gather(first_std, ("batch", "row"), axis=0, tiled=True),
            lax.all_gather(second_std, ("batch", "row"), axis=0, tiled=True),
            lax.all_gather(widen_std, ("batch", "row"), axis=0, tiled=True),
            lax.all_gather(squeeze_kernel, ("batch", "row"), axis=0, tiled=True),
            lax.all_gather(excite_kernel, ("batch", "row"), axis=0, tiled=True),
            lax.all_gather(narrow_bias, ("batch", "row"), axis=0, tiled=True),
            lax.all_gather(first_bias, ("batch", "row"), axis=0, tiled=True),
            lax.all_gather(second_bias, ("batch", "row"), axis=0, tiled=True),
            lax.all_gather(widen_bias, ("batch", "row"), axis=0, tiled=True),
            lax.all_gather(squeeze_bias, ("batch", "row"), axis=0, tiled=True),
            lax.all_gather(excite_bias, ("batch", "row"), axis=0, tiled=True),
        )
        output, input_grad, grads = micro_step(
            images[number], bucket[number], cotangent[number], shared, skip, leader, count
        )
        outputs.append(output)
        input_grads.append(input_grad)
        shares = (
            lax.psum_scatter(grads[0], ("batch", "row"), scatter_dimension=0, tiled=True),
            lax.psum_scatter(grads[1], ("batch", "row"), scatter_dimension=0, tiled=True),
            lax.psum_scatter(grads[2], ("batch", "row"), scatter_dimension=0, tiled=True),
            lax.psum_scatter(grads[3], ("batch", "row"), scatter_dimension=0, tiled=True),
            lax.psum_scatter(grads[4], ("batch", "row"), scatter_dimension=0, tiled=True),
            lax.psum_scatter(grads[5], ("batch", "row"), scatter_dimension=0, tiled=True),
            lax.psum_scatter(grads[6], ("batch", "row"), scatter_dimension=0, tiled=True),
            lax.psum_scatter(grads[7], ("batch", "row"), scatter_dimension=0, tiled=True),
            lax.psum_scatter(grads[8], ("batch", "row"), scatter_dimension=0, tiled=True),
            lax.psum_scatter(grads[9], ("batch", "row"), scatter_dimension=0, tiled=True),
            lax.psum_scatter(grads[10], ("batch", "row"), scatter_dimension=0, tiled=True),
            lax.psum_scatter(grads[11], ("batch", "row"), scatter_dimension=0, tiled=True),
            lax.psum_scatter(grads[12], ("batch", "row"), scatter_dimension=0, tiled=True),
        )
        summed = shares if summed is None else tuple_add(summed, shares)
    narrow_kernel_grad, narrow_gain_grad = jax.vjp(
        standard, narrow_kernel.astype(jnp.float32), narrow_gain.astype(jnp.float32)
    )[1](summed[0])
    first_kernel_grad, first_gain_grad = jax.vjp(
        standard, first_kernel.astype(jnp.float32), first_gain.astype(jnp.float32)
    )[1](summed[1])
    second_kernel_grad, second_gain_grad = jax.vjp(
        standard, second_kernel.astype(jnp.float32), second_gain.astype(jnp.float32)
    )[1](summed[2])
    widen_kernel_grad, widen_gain_grad = jax.vjp(
        standard, widen_kernel.astype(jnp.float32), widen_gain.astype(jnp.float32)
    )[1](summed[3])
    output_all = jnp.stack(outputs, axis=0)
    input_grad_all = jnp.stack(input_grads, axis=0)
    return (
        output_all,
        input_grad_all,
        narrow_kernel_grad,
        narrow_gain_grad,
        summed[6],
        first_kernel_grad,
        first_gain_grad,
        summed[7],
        second_kernel_grad,
        second_gain_grad,
        summed[8],
        widen_kernel_grad,
        widen_gain_grad,
        summed[9],
        summed[4],
        summed[10],
        summed[5],
        summed[11],
        summed[12],
    )


def solution(mesh):
    placed = (
        P(None, "batch", "row", None),
        P(None, "batch"),
        P(None, "batch", "row", None),
        P(("batch", "row"), None),
        P(("batch", "row")),
        P(("batch", "row")),
        P(("batch", "row"), None),
        P(("batch", "row")),
        P(("batch", "row")),
        P(("batch", "row"), None),
        P(("batch", "row")),
        P(("batch", "row")),
        P(("batch", "row"), None),
        P(("batch", "row")),
        P(("batch", "row")),
        P(("batch", "row"), None),
        P(("batch", "row")),
        P(("batch", "row"), None),
        P(("batch", "row")),
        P(),
    )
    return jax.shard_map(
        body,
        mesh=mesh,
        in_specs=placed,
        out_specs=(
            P(None, "batch", "row", None),
            P(None, "batch", "row", None),
            P(("batch", "row"), None),
            P(("batch", "row")),
            P(("batch", "row")),
            P(("batch", "row"), None),
            P(("batch", "row")),
            P(("batch", "row")),
            P(("batch", "row"), None),
            P(("batch", "row")),
            P(("batch", "row")),
            P(("batch", "row"), None),
            P(("batch", "row")),
            P(("batch", "row")),
            P(("batch", "row"), None),
            P(("batch", "row")),
            P(("batch", "row"), None),
            P(("batch", "row")),
            P(),
        ),
        check_vma=False,
    )
```

profile of v0, /device:TPU:0, one launch (start us, length us, event | category | flops | bytes accessed | tf_op | source)
XLA Modules:
  0.0 1099.7 jit_solution(15132526680832630729)
XLA Ops:
  34.7 42.5 %all-reduce.24 = (bf16[1536]{0:T(1024)(128)(2,1)S(1)}, bf16[768]{0:T(1024)(128)(2,1)S(1)}, bf16[768]{0:T(1024)(128)(2,1)S(1)}, bf16[768]{0:T(1024)(128)(2,1)S(1)...) all-reduce(bf16[1536]{0:T(1024)(128)(2,1)S(1)} %dynamic-update-slic, ...), channel_id=1, replica_groups=mesh['batch'=8,'row'=4] {'batch','row'}, use_global_device_ids=true, to_apply=%add.11 | all-reduce | flops 6144 | bytes 24576
  77.2 3.7 fusion.33
  84.1 3.9 multiply_convert_fusion.2
  90.0 3.9 collective-permute-start.4
  95.2 3.0 multiply_convert_fusion.5
  100.3 5.2 collective-permute-start
  126.7 7.9 copy.111
  134.6 6.8 reshape.966
  141.4 4.9 convolution_bitcast_fusion
  152.6 4.0 fusion.352
  174.7 7.9 copy.105
  182.5 6.8 reshape.957
  189.4 4.9 convolution_bitcast_fusion.1
  202.2 4.6 collective-permute-start.6
  208.1 4.6 collective-permute-start.2
  214.7 2.7 fusion.343
  218.5 2.8 collective-permute-done.3
  255.9 5.5 copy.115
  261.4 8.5 reshape.969
  275.4 7.9 copy.109
  283.2 6.8 reshape.960
  290.1 4.1 fusion.494
  298.8 2.8 convolution_add_fusion.4
  301.9 3.0 fusion.55
  307.9 2.7 copy.119
  310.6 3.6 reshape.974
  316.1 4.2 copy.120
  320.3 25.0 %all-reduce.28.cloned.1.call-done = (bf16[8,1536]{1,0:T(8,128)(2,1)}, bf16[8,1536]{1,0:T(8,128)(2,1)}, bf16[8,1536]{1,0:T(8,128)(2,1)}, bf16[8,1536]{1,0:T(8,128)(2,1)}) async-done(((bf16[8,1536]{1,0:T(8,128)(2,1)}, bf16[8,1536]{1,0:T(8,128)(2,1)}, bf16[8,1536]{1,0:T(8,128)(2,1)}, bf16[8,1536]{1,0:T(8,128)(2,1)}), (bf16[8,1536]{1,0:T(8,128)(2,1)}, bf16[8,1536]{1,0:T(8,128)(2,1)}, bf16[8,1536]{1,0:T(8,128)(2,1)}, ...) | async-done | bytes 98320 | tf_op jit(solution)/shard_map/psum | solution.py:145
  347.7 57.9 %all-gather.17.cloned.1.call-done = bf16[1536,768]{1,0:T(8,128)(2,1)} async-done(((bf16[48,768]{1,0:T(8,128)(2,1)}), bf16[1536,768]{1,0:T(8,128)(2,1)}) %all-gather.17.cloned.1.call-update) | async-done | bytes 2359312 | tf_op jit(solution)/shard_map/all_gather | solution.py:267
  405.6 3.2 fusion.428
  438.9 5.2 collective-permute-start.8
  466.3 8.0 copy.131
  474.3 8.5 reshape.981
  486.0 3.7 fusion.340
  500.0 5.5 copy.121
  505.5 7.2 reshape.977
  512.7 3.0 fusion.62
  515.7 5.8 fusion.474
  523.6 2.6 convolution_add_fusion.1
  530.0 3.6 reshape.973
  535.4 3.3 copy.118
  543.4 3.1 convolution_add_fusion.2
  556.1 3.0 fusion.106
  560.6 5.2 collective-permute-start.14
  572.7 4.5 collective-permute-start.10
  580.0 5.1 fusion.331
  596.5 2.6 fusion.206
  602.8 5.0 fusion.337
  628.3 4.1 select_dynamic-update-slice_fusion.2
  634.6 5.5 copy.127
  640.1 8.3 reshape.978
  648.4 4.2 convolution_multiply_fusion.7
  669.7 8.0 copy.137
  677.7 8.6 reshape.982
  686.3 4.3 convolution_multiply_fusion.4
  692.9 3.0 fusion.478
  697.1 3.0 convolution_add_fusion.3
  701.7 3.0 add_multiply_fusion
  706.3 3.0 add_multiply_fusion.1
  710.9 42.3 %all-reduce.23 = (f32[768]{0:T(1024)S(1)}, f32[768]{0:T(1024)S(1)}, f32[768]{0:T(1024)S(1)}, f32[1536]{0:T(1024)S(1)}, f32[768]{0:T(1024)S(1)}, /*index=5*/f32[1536]{0:T(1024)S(1)}, f32[32]{0:T(128)S(1)}) all-reduce(f32[768]{0:T(1024)S(1)} %add.1488, ...), channel_id=16, replica_groups=mesh['batch'=8,'row'=4] {'batch','row'}, use_global_device_ids=true, to_apply=%region_23.24.clone | all-reduce | flops 6176 | bytes 49408
  761.7 2.8 fusion.43
  777.9 89.8 %reduce-scatter.11.cloned.1.call-done = f32[24,1536]{1,0:T(8,128)} async-done(((f32[768,1536]{1,0:T(8,128)}), f32[24,1536]{1,0:T(8,128)}) %reduce-scatter.11.cloned.1.call-update) | async-done | bytes 147472 | tf_op jit(solution)/shard_map/reduce_scatter | solution.py:281
  871.2 109.3 %reduce-scatter.17.cloned.1.call-done = f32[48,768]{1,0:T(8,128)} async-done(((f32[1536,768]{1,0:T(8,128)}), f32[48,768]{1,0:T(8,128)}) %reduce-scatter.17.cloned.1.call-update) | async-done | bytes 147472 | tf_op jit(solution)/shard_map/reduce_scatter | solution.py:286
  980.5 112.1 %reduce-scatter.15.cloned.1.call-done = f32[24,1536]{1,0:T(8,128)} async-done(((f32[768,1536]{1,0:T(8,128)}), f32[24,1536]{1,0:T(8,128)}) %reduce-scatter.15.cloned.1.call-update) | async-done | bytes 147472 | tf_op jit(solution)/shard_map/reduce_scatter | solution.py:285
  (764 shorter events, 329.2 us)
Async XLA Ops:
  7.2 73.8 %copy-start.193 = (s32[2,8]{1,0:T(2,128)S(1)}, s32[2,8]{1,0:T(2,128)}, u32[]{:S(2)}) copy-start(s32[2,8]{1,0:T(2,128)} %param.21) | copy-start | bytes 196
  7.2 76.9 %all-gather.11.cloned.1.call-start = ((), (), s32[]{:S(2)}) async-start(), calls=%async_computation.8 | async-start | bytes 2433024 | tf_op jit(solution)/shard_map/all_gather | solution.py:262
  12.8 128.6 %all-gather.9.cloned.1.call-start = ((), (), s32[]{:S(2)}) async-start(), calls=%async_computation.7 | async-start | bytes 1824768 | tf_op jit(solution)/shard_map/all_gather | solution.py:263
  18.1 272.0 %all-gather.7.cloned.1.call-start = ((), (), s32[]{:S(2)}) async-start(), calls=%async_computation.6 | async-start | bytes 1824768 | tf_op jit(solution)/shard_map/all_gather | solution.py:264
  23.4 275.4 %all-gather.13.cloned.1.call-start = ((), (), s32[]{:S(2)}) async-start(), calls=%async_computation.9 | async-start | bytes 2433024 | tf_op jit(solution)/shard_map/all_gather | solution.py:265
  28.9 291.4 %all-gather.15.cloned.1.call-start = ((), (), s32[]{:S(2)}) async-start(), calls=%async_computation.10 | async-start | bytes 2433024 | tf_op jit(solution)/shard_map/all_gather | solution.py:266
  29.5 315.8 %all-reduce.28.cloned.1.call-start = ((), (), s32[]{:S(2)}) async-start(), calls=%async_computation.18 | async-start | bytes 196608 | tf_op jit(solution)/shard_map/psum | solution.py:145
  77.2 10.8 copy-start.188
  81.0 136.4 %copy-start.132 = (pred[8]{0:T(512)(128)(4,1)}, pred[8]{0:T(512)(128)(4,1)S(1)}, u32[]{:S(2)}) copy-start(pred[8]{0:T(512)(128)(4,1)S(1)} %get-tuple-element.191) | copy-start | bytes 28
  81.0 150.5 %copy-start.130 = (pred[8]{0:T(512)(128)(4,1)}, pred[8]{0:T(512)(128)(4,1)S(1)}, u32[]{:S(2)}) copy-start(pred[8]{0:T(512)(128)(4,1)S(1)} %get-tuple-element.190) | copy-start | bytes 28
  84.1 166.1 %copy-start.126 = (pred[8,32]{1,0:T(8,128)(4,1)}, pred[8,32]{1,0:T(8,128)(4,1)S(1)}, u32[]{:S(2)}) copy-start(pred[8,32]{1,0:T(8,128)(4,1)S(1)} %get-tuple-element.189) | copy-start | bytes 772
  84.1 11.1 %copy-start.22 = (bf16[768,1536]{1,0:T(8,128)(2,1)S(1)}, bf16[768,1536]{1,0:T(8,128)(2,1)}, u32[]{:S(2)}) copy-start(bf16[768,1536]{1,0:T(8,128)(2,1)} %all-gather.11.cloned.1.call-done) | copy-start | bytes 7077892
  90.0 17.0 %collective-permute-start.4 = (bf16[8,16,768]{2,1,0:T(8,128)(2,1)}, bf16[8,16,768]{2,1,0:T(8,128)(2,1)S(1)}, u32[]{:S(2)}, u32[]{:S(2)}) collective-permute-start(bf16[8,16,768]{2,1,0:T(8,128)(2,1)} %get-tuple-element.157), channel_id=1, source_target_pairs={{0,1},{1,2},{2,3},{4,5},{5,6},{6,7},{8,9},{9,10},{10,11},{12,13},{... | collective-permute-start | bytes 589832 | tf_op jit(solution)/shard_map/ppermute | solution.py:21
  93.9 13.1 %collective-permute-start.5 = (bf16[8,16,768]{2,1,0:T(8,128)(2,1)}, bf16[8,16,768]{2,1,0:T(8,128)(2,1)S(1)}, u32[]{:S(2)}, u32[]{:S(2)}) collective-permute-start(bf16[8,16,768]{2,1,0:T(8,128)(2,1)} %get-tuple-element.156), channel_id=1, source_target_pairs={{1,0},{2,1},{3,2},{5,4},{6,5},{7,6},{9,8},{10,9},{11,10},{13,12},{... | collective-permute-start | bytes 589832 | tf_op jit(solution)/shard_map/ppermute | solution.py:24
  98.3 11.4 %copy-start.17 = (bf16[256,768]{1,0:T(8,128)(2,1)}, bf16[256,768]{1,0:T(8,128)(2,1)S(1)}, u32[]{:S(2)}) copy-start(bf16[256,768]{1,0:T(8,128)(2,1)S(1)} %get-tuple-element.192) | copy-start | bytes 1179652
  98.3 9.0 copy-start.150
  98.3 9.0 copy-start.153
  100.3 50.8 %collective-permute-start = (bf16[8,16,768]{2,1,0:T(8,128)(2,1)}, bf16[8,16,768]{2,1,0:T(8,128)(2,1)}, u32[]{:S(2)}, u32[]{:S(2)}) collective-permute-start(bf16[8,16,768]{2,1,0:T(8,128)(2,1)} %get-tuple-element.153), channel_id=1, source_target_pairs={{0,1},{1,2},{2,3},{4,5},{5,6},{6,7},{8,9},{9,10},{10,11},{12,13},{... | collective-permute-start | bytes 589832 | tf_op jit(solution)/shard_map/ppermute | solution.py:21
  105.5 45.6 %collective-permute-start.1 = (bf16[8,16,768]{2,1,0:T(8,128)(2,1)}, bf16[8,16,768]{2,1,0:T(8,128)(2,1)}, u32[]{:S(2)}, u32[]{:S(2)}) collective-permute-start(bf16[8,16,768]{2,1,0:T(8,128)(2,1)} %get-tuple-element.152), channel_id=1, source_target_pairs={{1,0},{2,1},{3,2},{5,4},{6,5},{7,6},{9,8},{10,9},{11,10},{13,12},{... | collective-permute-start | bytes 589832 | tf_op jit(solution)/shard_map/ppermute | solution.py:24
  198.1 52.1 %copy-start.31 = (f32[256,6,128]{2,0,1:T(8,128)}, f32[256,6,128]{2,0,1:T(8,128)S(1)}, u32[]{:S(2)}) copy-start(f32[256,6,128]{2,0,1:T(8,128)S(1)} %copy.107) | copy-start | bytes 2359300
  201.5 13.1 %copy-start.35 = (f32[8,32,768]{2,1,0:T(8,128)}, f32[8,32,768]{2,1,0:T(8,128)S(1)}, u32[]{:S(2)}) copy-start(f32[8,32,768]{2,1,0:T(8,128)S(1)} %reshape.958) | copy-start | bytes 2359300
  201.6 13.1 %copy-start.151 = (pred[8,32]{1,0:T(8,128)(4,1)S(1)}, pred[8,32]{1,0:T(8,128)(4,1)}, u32[]{:S(2)}) copy-start(pred[8,32]{1,0:T(8,128)(4,1)} %get-tuple-element.185) | copy-start | bytes 772
  201.6 13.1 %copy-start.154 = (pred[8,32]{1,0:T(8,128)(4,1)S(1)}, pred[8,32]{1,0:T(8,128)(4,1)}, u32[]{:S(2)}) copy-start(pred[8,32]{1,0:T(8,128)(4,1)} %get-tuple-element.187) | copy-start | bytes 772
  202.2 11.8 %collective-permute-start.6 = (bf16[8,16,768]{2,1,0:T(8,128)(2,1)S(1)}, bf16[8,16,768]{2,1,0:T(8,128)(2,1)S(1)}, u32[]{:S(2)}, u32[]{:S(2)}) collective-permute-start(bf16[8,16,768]{2,1,0:T(8,128)(2,1)S(1)} %get-tuple-element.155), channel_id=1, source_target_pairs={{0,1},{1,2},{2,3},{4,5},{5,6},{6,7},{8,9},{9,10},{10,11},{12,13},{... | collective-permute-start | bytes 589832 | tf_op jit(solution)/shard_map/ppermute | solution.py:21
  206.8 7.6 collective-permute-start.7
  208.1 10.3 collective-permute-start.2
  212.7 8.6 collective-permute-start.3
  222.8 8.7 copy-start.145
  222.8 8.7 copy-start.148
  234.1 9.4 copy-start.83
  261.4 8.5 copy-start.86
  261.4 8.9 copy-start.85
  261.4 9.4 copy-start.82
  305.0 100.6 %all-gather.17.cloned.1.call-start = ((), (), s32[]{:S(2)}) async-start(), calls=%async_computation.11 | async-start | bytes 2433024 | tf_op jit(solution)/shard_map/all_gather | solution.py:267
  305.7 461.6 %reduce-scatter.21.cloned.1.call-start = ((), (), s32[]{:S(2)}) async-start(), calls=%async_computation.17 | async-start | bytes 3649536
  345.3 60.3 %copy-start.117 = (bf16[8,1536]{1,0:T(8,128)(2,1)S(1)}, bf16[8,1536]{1,0:T(8,128)(2,1)}, u32[]{:S(2)}) copy-start(bf16[8,1536]{1,0:T(8,128)(2,1)} %get-tuple-element.54) | copy-start | bytes 73732
  347.7 62.1 %copy-start.111 = (f32[8,768]{1,0:T(8,128)}, f32[8,768]{1,0:T(8,128)S(1)}, u32[]{:S(2)}) copy-start(f32[8,768]{1,0:T(8,128)S(1)} %convolution_add_fusion.10) | copy-start | bytes 73732
  433.4 12.1 %copy-start.133 = (pred[8]{0:T(512)(128)(4,1)S(1)}, pred[8]{0:T(512)(128)(4,1)}, u32[]{:S(2)}) copy-start(pred[8]{0:T(512)(128)(4,1)} %copy-done.132) | copy-start | bytes 28
  433.4 337.4 %reduce-scatter.19.cloned.1.call-start = ((), (), s32[]{:S(2)}) async-start(), calls=%async_computation.16 | async-start | bytes 3649536
  434.4 11.0 collective-permute-start.12
  436.8 8.7 collective-permute-start.13
  438.1 8.4 copy-start.152
  438.1 8.4 copy-start.155
  438.9 43.9 %collective-permute-start.8 = (bf16[8,16,768]{2,1,0:T(8,128)(2,1)}, bf16[8,16,768]{2,1,0:T(8,128)(2,1)}, u32[]{:S(2)}, u32[]{:S(2)}) collective-permute-start(bf16[8,16,768]{2,1,0:T(8,128)(2,1)} %get-tuple-element.145), channel_id=1, source_target_pairs={{0,1},{1,2},{2,3},{4,5},{5,6},{6,7},{8,9},{9,10},{10,11},{12,13},{... | collective-permute-start | bytes 589832 | tf_op jit(solution)/shard_map/ppermute | solution.py:21
  444.1 38.7 %collective-permute-start.9 = (bf16[8,16,768]{2,1,0:T(8,128)(2,1)}, bf16[8,16,768]{2,1,0:T(8,128)(2,1)}, u32[]{:S(2)}, u32[]{:S(2)}) collective-permute-start(bf16[8,16,768]{2,1,0:T(8,128)(2,1)} %get-tuple-element.144), channel_id=1, source_target_pairs={{1,0},{2,1},{3,2},{5,4},{6,5},{7,6},{9,8},{10,9},{11,10},{13,12},{... | collective-permute-start | bytes 589832 | tf_op jit(solution)/shard_map/ppermute | solution.py:24
  474.3 8.5 copy-start.127
  474.3 8.5 copy-start.131
  526.2 248.1 %reduce-scatter.13.cloned.1.call-start = ((), (), s32[]{:S(2)}) async-start(), calls=%async_computation.13 | async-start | bytes 4866048 | tf_op jit(solution)/shard_map/reduce_scatter | solution.py:284
  546.5 321.2 %reduce-scatter.11.cloned.1.call-start = ((), (), s32[]{:S(2)}) async-start(), calls=%async_computation.12 | async-start | bytes 4866048 | tf_op jit(solution)/shard_map/reduce_scatter | solution.py:281
  560.6 17.9 %collective-permute-start.14 = (bf16[8,16,768]{2,1,0:T(8,128)(2,1)}, bf16[8,16,768]{2,1,0:T(8,128)(2,1)}, u32[]{:S(2)}, u32[]{:S(2)}) collective-permute-start(bf16[8,16,768]{2,1,0:T(8,128)(2,1)} %get-tuple-element.147), channel_id=1, source_target_pairs={{0,1},{1,2},{2,3},{4,5},{5,6},{6,7},{8,9},{9,10},{10,11},{12,13},{... | collective-permute-start | bytes 589832 | tf_op jit(solution)/shard_map/ppermute | solution.py:21
  565.9 12.7 %collective-permute-start.15 = (bf16[8,16,768]{2,1,0:T(8,128)(2,1)}, bf16[8,16,768]{2,1,0:T(8,128)(2,1)}, u32[]{:S(2)}, u32[]{:S(2)}) collective-permute-start(bf16[8,16,768]{2,1,0:T(8,128)(2,1)} %get-tuple-element.146), channel_id=1, source_target_pairs={{1,0},{2,1},{3,2},{5,4},{6,5},{7,6},{9,8},{10,9},{11,10},{13,12},{... | collective-permute-start | bytes 589832 | tf_op jit(solution)/shard_map/ppermute | solution.py:24
  572.7 23.8 %collective-permute-start.10 = (bf16[8,16,768]{2,1,0:T(8,128)(2,1)}, bf16[8,16,768]{2,1,0:T(8,128)(2,1)S(1)}, u32[]{:S(2)}, u32[]{:S(2)}) collective-permute-start(bf16[8,16,768]{2,1,0:T(8,128)(2,1)} %get-tuple-element.143), channel_id=1, source_target_pairs={{0,1},{1,2},{2,3},{4,5},{5,6},{6,7},{8,9},{9,10},{10,11},{12,13},{... | collective-permute-start | bytes 589832 | tf_op jit(solution)/shard_map/ppermute | solution.py:21
  577.2 19.3 %collective-permute-start.11 = (bf16[8,16,768]{2,1,0:T(8,128)(2,1)}, bf16[8,16,768]{2,1,0:T(8,128)(2,1)}, u32[]{:S(2)}, u32[]{:S(2)}) collective-permute-start(bf16[8,16,768]{2,1,0:T(8,128)(2,1)} %get-tuple-element.142), channel_id=1, source_target_pairs={{1,0},{2,1},{3,2},{5,4},{6,5},{7,6},{9,8},{10,9},{11,10},{13,12},{... | collective-permute-start | bytes 589832 | tf_op jit(solution)/shard_map/ppermute | solution.py:24
  700.1 280.5 %reduce-scatter.17.cloned.1.call-start = ((), (), s32[]{:S(2)}) async-start(), calls=%async_computation.15 | async-start | bytes 4866048 | tf_op jit(solution)/shard_map/reduce_scatter | solution.py:286
  704.7 388.0 %reduce-scatter.15.cloned.1.call-start = ((), (), s32[]{:S(2)}) async-start(), calls=%async_computation.14 | async-start | bytes 4866048 | tf_op jit(solution)/shard_map/reduce_scatter | solution.py:285
  765.9 8.4 copy-start.51
  765.9 8.4 copy-start.163
  765.9 8.4 copy-start.176
  766.0 10.0 copy-start.199
  766.0 101.7 %copy-start.52 = (bf16[24,1536]{1,0:T(8,128)(2,1)S(1)}, bf16[24,1536]{1,0:T(8,128)(2,1)}, u32[]{:S(2)}) copy-start(bf16[24,1536]{1,0:T(8,128)(2,1)} %param.23) | copy-start | bytes 221188
  766.0 101.7 %copy-start.159 = (f32[24]{0:T(128)S(1)}, f32[24]{0:T(128)}, u32[]{:S(2)}) copy-start(f32[24]{0:T(128)} %copy-done.158) | copy-start | bytes 292
  766.0 101.7 %copy-start.168 = (f32[24]{0:T(128)S(1)}, f32[24]{0:T(128)}, u32[]{:S(2)}) copy-start(f32[24]{0:T(128)} %copy-done.167) | copy-start | bytes 292
  766.0 101.7 %copy-start.170 = (f32[24]{0:T(128)S(1)}, f32[24]{0:T(128)}, u32[]{:S(2)}) copy-start(f32[24]{0:T(128)} %copy-done.169) | copy-start | bytes 292
  766.0 103.3 %copy-start.195 = (f32[24]{0:T(128)S(1)}, f32[24]{0:T(128)}, u32[]{:S(2)}) copy-start(f32[24]{0:T(128)} %copy-done.194) | copy-start | bytes 292
  (170 other events, 476.4 us)
Sparse Core Ops, SparseCore 0:
  12.9 60.2 all-gather.10
  76.6 54.4 all-gather.8
  134.6 54.6 all-gather.6
  192.5 56.4 all-gather.12
  251.6 56.2 all-gather.14
  312.0 33.2 all-reduce.27
  348.5 57.0 all-gather.16
  433.5 101.8 reduce-scatter.20
  541.8 102.0 reduce-scatter.18
  650.1 105.9 reduce-scatter.12
  761.6 106.0 reduce-scatter.10
  874.5 106.0 reduce-scatter.16
  986.6 106.0 reduce-scatter.14
where the time goes:
time: 1110 us; the launch traced here: 1100 us
  waiting for transfers between devices  399 us (36%)
  local copies, waits for them, and re-layouts  353 us (32%)
  other arithmetic  110 us (10%)
  matrix products  87 us (8%)
  blocking collectives  84.8 us (8%)
  starting transfers between devices  46.8 us (4%)
  between operations  19.2 us (2%)
    another operation x80, local copies, waits for them, and re-layouts, columns(): stacked = jnp.stack(pieces, axis=3)  148 us
    reduce_scatter x1, waiting for transfers between devices, body(): lax.psum_scatter(grads[4], ('batch', 'row'), scatter_dimension=0, tiled=T...  112 us
    reduce_scatter x1, waiting for transfers between devices, body(): lax.psum_scatter(grads[5], ('batch', 'row'), scatter_dimension=0, tiled=T...  109 us
    reduce_scatter x1, waiting for transfers between devices, body(): lax.psum_scatter(grads[0], ('batch', 'row'), scatter_dimension=0, tiled=T...  89.8 us
    unnamed x2, blocking collectives  84.8 us
    unnamed x485, local copies, waits for them, and re-layouts  74.8 us
    reshape x8, local copies, waits for them, and re-layouts, columns(): return stacked.reshape(blocks * strip, groups, 9 * GW)  61.4 us
    all_gather x1, waiting for transfers between devices, body(): lax.all_gather(excite_kernel, ('batch', 'row'), axis=0, tiled=True)  57.9 us
  transfers between devices with their start and end apart: 29, of which 8 were waited for; matrix products, arithmetic and copies ran while one was open for 45% of the time, Pallas kernels for 0%

commit v1 on v0

v1 whole, which is shorter than its diff:
```python
import functools
import math
import types

import jax
import jax.numpy as jnp
from jax import lax
from jax.experimental import pallas as pl
from jax.experimental.pallas import tpu as pltpu
from jax.sharding import PartitionSpec as P

MESH = pl.DeviceIdType.MESH
BF = jnp.bfloat16
F32 = jnp.float32

GW = 128
PIX = 128
TAPS = 9
gamma_act = 1.7015
alpha_res = 0.2
beta_in = 0.9622504486493763
eps_std = 0.0001
tanh_scale = math.sqrt(2.0 / math.pi)
tanh_cube = 0.044715

NN = ((1,), (0,))
NT = ((1,), (1,))
TN = ((0,), (0,))


def dot(left, right, dims):
    return lax.dot_general(left, right, (dims, ((), ())), preferred_element_type=F32)


def place():
    return lax.axis_index("batch"), lax.axis_index("row")


def flip(value, bit):
    return lax.bitwise_xor(value, jnp.int32(bit))


def tile(index, size):
    return pl.ds(pl.multiple_of(index * size, size), size)


def greet(everywhere):
    b, z = place()
    barrier = pltpu.get_barrier_semaphore()
    for bit in (1, 2, 3):
        pl.semaphore_signal(barrier, inc=1, device_id=(b, flip(z, bit)), device_id_type=MESH)
    if everywhere:
        for bit in (1, 2, 4):
            pl.semaphore_signal(barrier, inc=1, device_id=(flip(b, bit), z), device_id_type=MESH)
    pl.semaphore_wait(barrier, 6 if everywhere else 3)


class Transfer:
    def __init__(self, send, recv):
        self.send, self.recv, self.copies = send, recv, {}

    def copy(self, key, src, dst, device):
        made = pltpu.make_async_remote_copy(
            src_ref=src, dst_ref=dst, send_sem=self.send.at[key], recv_sem=self.recv.at[key],
            device_id=device, device_id_type=MESH)
        made.start()
        self.copies[key] = made

    def arrived(self, *keys):
        for key in keys:
            self.copies[key].wait_recv()

    def close(self):
        for made in self.copies.values():
            made.wait_send()


class Gather(Transfer):
    def __init__(self, slots, whole, send, recv, halves=True, block=None):
        super().__init__(send, recv)
        self.slots, self.whole, self.halves = slots, whole, halves
        self.rows = slots.shape[1]
        self.block = 4 * self.rows if block is None else block
        self.half = self.block // 2

    def at(self, index, start=0, size=None):
        size = self.block if size is None else size
        return self.whole.at[pl.ds(pl.multiple_of(index * self.block + start, 8 if self.rows == 8 else 16), size)]

    def along_row(self):
        b, z = place()
        for j in (1, 2, 3):
            self.copy(j - 1, self.slots.at[z], self.slots.at[z], (b, flip(z, j)))

    def assemble(self):
        b, z = place()
        base = pl.multiple_of(b * self.block, 16)
        if self.rows % 16 == 0:
            for r in range(4):
                self.whole[pl.ds(base + r * self.rows, self.rows)] = self.slots[r]
        else:
            for r in (0, 2):
                pair = jnp.concatenate([self.slots[r].astype(F32), self.slots[r + 1].astype(F32)], axis=0)
                self.whole[pl.ds(base + r * self.rows, 2 * self.rows)] = pair.astype(self.whole.dtype)

    def own_block(self):
        b, z = place()
        self.arrived(0, 1, 2)
        self.assemble()
        own = self.at(b)
        self.copy(3, own, own, (flip(b, 2), z))
        self.copy(4, own, own, (flip(b, 4), z))
        self.copy(5, own, own, (flip(b, 1), z))

    def onward(self):
        b, z = place()
        self.arrived(3)
        low = self.at(flip(b, 2), 0, self.half) if self.halves else self.at(flip(b, 2))
        self.copy(6, low, low, (flip(b, 4), z))
        near = self.at(flip(b, 2))
        self.copy(8, near, near, (flip(b, 1), z))
        self.arrived(4)
        if self.halves:
            high = self.at(flip(b, 4), self.half, self.half)
            self.copy(7, high, high, (flip(b, 2), z))
        near = self.at(flip(b, 4))
        self.copy(9, near, near, (flip(b, 1), z))

    def corner(self):
        b, z = place()
        self.arrived(6)
        if self.halves:
            self.arrived(7)
        far = self.at(flip(b, 6))
        self.copy(10, far, far, (flip(b, 1), z))

    def ready(self):
        self.arrived(5, 8, 9, 10)


class Factors(Gather):
    def assemble(self):
        b, z = place()
        width = self.slots.shape[2]
        columns = []
        for q in range(4):
            rows = [self.slots[r].astype(F32)[4 * q:4 * q + 4] for r in range(4)]
            columns.append(jnp.concatenate(rows, axis=0))
        self.whole[pl.ds(pl.multiple_of(b * 16, 16), 16)] = jnp.concatenate(columns, axis=1).astype(BF)


class Scatter(Transfer):
    def __init__(self, whole, mate, diagonal, sides, pieces, landed, send, recv):
        super().__init__(send, recv)
        self.whole, self.mate, self.diagonal, self.sides = whole, mate, diagonal, sides
        self.pieces, self.landed = pieces, landed
        self.rows = pieces.shape[1]
        self.block = 4 * self.rows
        self.half = self.block // 2

    def at(self, index, start=0, size=None):
        size = self.block if size is None else size
        return self.whole.at[pl.ds(pl.multiple_of(index * self.block + start, 16), size)]

    def to_mate(self):
        b, z = place()
        for k, q in enumerate((6, 2, 4, 0)):
            self.copy(k, self.at(flip(b, 1 ^ q)), self.mate.at[k], (flip(b, 1), z))

    def add(self, index, start, size, ref):
        where = pl.ds(pl.multiple_of(index * self.block + start, 16), size)
        total = self.whole[where].astype(F32) + ref[...].astype(F32)
        self.whole[where] = total.astype(self.whole.dtype)

    def diagonals(self):
        b, z = place()
        self.arrived(0)
        self.add(flip(b, 6), 0, self.block, self.mate.at[0])
        self.copy(4, self.at(flip(b, 6), 0, self.half), self.diagonal.at[0], (flip(b, 4), z))
        self.copy(5, self.at(flip(b, 6), self.half, self.half), self.diagonal.at[1], (flip(b, 2), z))
        self.arrived(1)
        self.add(flip(b, 2), 0, self.block, self.mate.at[1])
        self.arrived(2)
        self.add(flip(b, 4), 0, self.block, self.mate.at[2])
        self.arrived(3)
        self.add(b, 0, self.block, self.mate.at[3])

    def to_sides(self):
        b, z = place()
        self.arrived(4)
        self.add(flip(b, 2), 0, self.half, self.diagonal.at[0])
        self.copy(6, self.at(flip(b, 2)), self.sides.at[0], (flip(b, 2), z))
        self.arrived(5)
        self.add(flip(b, 4), self.half, self.half, self.diagonal.at[1])
        self.copy(7, self.at(flip(b, 4)), self.sides.at[1], (flip(b, 4), z))

    def along_row(self):
        b, z = place()
        self.arrived(6, 7)
        step = 1 if self.rows % 16 == 0 else 2
        size = step * self.rows
        for r in range(0, 4, step):
            start = r * self.rows
            part = self.whole[pl.ds(pl.multiple_of(b * self.block + start, 16), size)].astype(F32)
            for side in (0, 1):
                part += self.sides[side, start:start + size].astype(F32)
            for k in range(step):
                self.pieces[r + k] = part[k * self.rows:(k + 1) * self.rows].astype(self.pieces.dtype)
        for j in (1, 2, 3):
            self.copy(7 + j, self.pieces.at[flip(z, j)], self.landed.at[j - 1], (b, flip(z, j)))

    def total(self):
        b, z = place()
        result = self.pieces[z].astype(F32)
        for j in (1, 2, 3):
            self.arrived(7 + j)
            result += self.landed[j - 1].astype(F32)
        return result


class Halo:
    def __init__(self, field, send, recv, blocks):
        self.field, self.send, self.recv, self.blocks = field, send, recv, blocks

    def made(self, part, way):
        b, z = place()
        images = pl.ds(part * self.blocks, self.blocks)
        source, target, step = ((32, 0, 1), (16, 48, -1))[way]
        return pltpu.make_async_remote_copy(
            src_ref=self.field.at[images, pl.ds(source, 16)], dst_ref=self.field.at[images, pl.ds(target, 16)],
            send_sem=self.send.at[part, way], recv_sem=self.recv.at[part, way],
            device_id=(b, z + step), device_id_type=MESH)

    def each(self, part, low, high, act):
        b, z = place()

        @pl.when(z < 3)
        def _():
            act(self.made(part, low))

        @pl.when(z > 0)
        def _():
            act(self.made(part, high))

    def start(self, part):
        self.each(part, 0, 1, lambda made: made.start())

    def arrived(self, part):
        self.each(part, 1, 0, lambda made: made.wait_recv())

    def close(self, part):
        self.each(part, 0, 1, lambda made: made.wait_send())


def act_only(value):
    inner = jnp.tanh(tanh_scale * value * (1.0 + tanh_cube * (value * value)))
    return (0.5 * gamma_act) * value * (1.0 + inner)


def gelu_pair(value, scale):
    square = value * value
    inner = jnp.tanh(tanh_scale * value * (1.0 + tanh_cube * square))
    half = 0.5 + 0.5 * inner
    slope = half + (0.5 * tanh_scale) * value * (1.0 - inner * inner) * (1.0 + (3.0 * tanh_cube) * square)
    return scale * value * half, scale * slope


def column(row, count):
    lanes = lax.broadcasted_iota(jnp.int32, (count, 128), 1)
    ups = lax.broadcasted_iota(jnp.int32, (count, 128), 0)
    return jnp.sum(jnp.where(lanes == ups, row, 0.0), axis=1, keepdims=True)


def as_row(col, count):
    lanes = lax.broadcasted_iota(jnp.int32, (count, 128), 1)
    ups = lax.broadcasted_iota(jnp.int32, (count, 128), 0)
    return jnp.sum(jnp.where(lanes == ups, col, 0.0), axis=0, keepdims=True)


def centred(kernel_ref):
    kernel = kernel_ref[...].astype(F32)
    fan = kernel.shape[1]
    center = kernel - jnp.mean(kernel, axis=1, keepdims=True)
    spread = jnp.mean(center * center, axis=1, keepdims=True)
    return center, lax.rsqrt(fan * spread + eps_std)


def standard(kernel_ref, gain):
    center, scale = centred(kernel_ref)
    return gain * center * scale


def standard_back(kernel_ref, gain, cotan):
    center, scale = centred(kernel_ref)
    along = jnp.sum(cotan * center, axis=1, keepdims=True)
    mean = jnp.mean(cotan, axis=1, keepdims=True)
    kernel_grad = (gain * scale) * (cotan - mean) - (gain * along * scale * scale * scale) * center
    return kernel_grad, along * scale


def owners(devices, share, width):
    place_of = lax.broadcasted_iota(jnp.int32, (128, width), 1).astype(F32)
    within = place_of - share * jnp.floor((place_of + 0.5) * (1.0 / share))
    slot = lax.broadcasted_iota(jnp.int32, (128, width), 0).astype(F32)
    pick = jnp.where(within == slot, 1.0, 0.0).astype(BF)
    index = lax.broadcasted_iota(jnp.int32, (devices, width), 1)
    owner = lax.broadcasted_iota(jnp.int32, (devices, width), 0)
    mine = (index >= owner * share) & (index < owner * share + share)
    return pick, mine


def from_shares(shares, share, width):
    pick, mine = owners(shares.shape[0], share, width)
    spread = dot(shares.astype(BF), pick, NN)
    return jnp.sum(jnp.where(mine, spread, 0.0), axis=0, keepdims=True)


def to_shares(row, devices, share):
    pick, mine = owners(devices, share, row.shape[1])
    masked = jnp.where(mine, row, 0.0)
    upper = masked.astype(BF)
    lower = (masked - upper.astype(F32)).astype(BF)
    return dot(upper, pick, NT) + dot(lower, pick, NT)


def build_columns(field, cols, bucket, part, blocks, reverse):
    width = field.shape[2]

    def body(i, carry):
        image = part * blocks + i
        value = field[image].astype(F32)
        size = jnp.where(bucket[part, i] == 0, 16, 8)
        place_in = jnp.bitwise_and(lax.broadcasted_iota(jnp.int32, (64, width), 0), size - 1)
        left = jnp.where(place_in != 0, pltpu.roll(value, 1, 0), 0.0)
        right = jnp.where(place_in != size - 1, pltpu.roll(value, 63, 0), 0.0)
        wide = jnp.full((32, width), size, jnp.int32) == 16
        for step_col, moved in ((-1, left), (0, value), (1, right)):
            for step_row in (-1, 0, 1):
                if step_row == 0:
                    tap = moved[16:48]
                elif step_row == -1:
                    tap = jnp.where(wide, moved[0:32], moved[8:40])
                else:
                    tap = jnp.where(wide, moved[32:64], moved[24:56])
                t = (step_row + 1) * 3 + step_col + 1
                t = 8 - t if reverse else t
                tap = tap.astype(BF)
                rows = pl.ds(pl.multiple_of(image * 32, 32), 32)
                for g in range(width // GW):
                    cols[g, rows, t * GW:(t + 1) * GW] = tap[:, g * GW:(g + 1) * GW]
        return carry

    lax.fori_loop(0, blocks, body, 0)


def narrow_part(ns, part):
    rows = tile(part, ns.strip)
    images = pl.ds(part * ns.blocks, ns.blocks)

    def body(n, carry):
        lanes = tile(n, 256)
        value = dot(ns.act0[rows, :], ns.w[0][lanes, :], NT) + ns.brow[0:1, lanes]
        act, slope = gelu_pair(value, gamma_act)
        ns.slope0[rows, lanes] = slope.astype(BF)
        ns.ext1[images, 16:48, lanes] = act.reshape(ns.blocks, 32, 256).astype(BF)
        return carry

    lax.fori_loop(0, ns.mid // 256, body, 0)


def group_part(ns, part, which, target, slope_ref):
    rows = tile(part, ns.strip)
    images = pl.ds(part * ns.blocks, ns.blocks)

    def body(g, carry):
        lanes = tile(g, GW)
        value = dot(ns.cols[g, rows, :], ns.w[which][lanes, :], NT) + ns.brow[which:which + 1, lanes]
        act, slope = gelu_pair(value, gamma_act)
        slope_ref[rows, lanes] = slope.astype(BF)
        if target is ns.act3:
            target[rows, lanes] = act.astype(BF)
        else:
            target[images, 16:48, lanes] = act.reshape(ns.blocks, 32, GW).astype(BF)
        return carry

    lax.fori_loop(0, ns.mid // GW, body, 0)


def widen_part(ns, part):
    rows = tile(part, ns.strip)

    def body(n, carry):
        lanes = tile(n, 256)
        branch = dot(ns.act3[rows, :], ns.w[3][lanes, :], NT) + ns.brow[3:4, lanes]
        ns.out[rows, lanes] = branch.astype(BF)
        upstream = ns.cotangent[rows, lanes].astype(F32)
        images = tile(part, ns.blocks)
        ns.sums[0, images, lanes] = jnp.sum(branch.reshape(ns.blocks, 32, 256), axis=1)
        ns.sums[1, images, lanes] = jnp.sum((branch * upstream).reshape(ns.blocks, 32, 256), axis=1)
        return carry

    lax.fori_loop(0, ns.width // 256, body, 0)


def send_sums(ns):
    b, z = place()
    half = ns.width // 2
    for r in range(4):
        parts = [ns.sums[kind, 4 * r:4 * r + 4, side * half:(side + 1) * half] for kind in (0, 1) for side in (0, 1)]
        ns.shared_out[r] = jnp.concatenate(parts, axis=0).astype(BF)
    for j in (1, 2, 3):
        ns.pool.copy(j - 1, ns.shared_out.at[flip(z, j)], ns.shared_in.at[j - 1], (b, flip(z, j)))


def excite_images(ns):
    b, z = place()
    total = ns.shared_out[z].astype(F32)
    for j in (1, 2, 3):
        ns.pool.arrived(j - 1)
        total += ns.shared_in[j - 1].astype(F32)
    pad = jnp.zeros((12, ns.width), F32)
    pooled = jnp.concatenate([total[0:4], total[4:8]], axis=1) * (1.0 / PIX)
    along = jnp.concatenate([total[8:12], total[12:16]], axis=1)
    pooled = jnp.concatenate([pooled, pad], axis=0).astype(BF)
    along = alpha_res * jnp.concatenate([along, pad], axis=0)
    squeezed = dot(pooled, ns.w[4][...], NT) + ns.brow[4:5, 0:ns.mid]
    hidden, slope = gelu_pair(squeezed, 1.0)
    hidden = hidden.astype(BF)
    excited = dot(hidden, ns.w[5][...], NT) + ns.brow[5:6, :]
    sigmoid = jax.nn.sigmoid(excited)
    gate = 2.0 * sigmoid
    excited_grad = (ns.skip * along) * (gate * (1.0 - sigmoid))
    excited_low = excited_grad.astype(BF)
    squeezed_grad = dot(excited_low, ns.w[5][...], NN) * slope
    squeezed_low = squeezed_grad.astype(BF)
    pooled_grad = dot(squeezed_low, ns.w[4][...], NN) * (1.0 / PIX)
    half = ns.width // 2
    parts = [value[0:4, side * half:(side + 1) * half] for value in (gate, pooled_grad) for side in (0, 1)]
    ns.shared_back[z] = jnp.concatenate(parts, axis=0).astype(BF)
    for j in (1, 2, 3):
        ns.back.copy(j - 1, ns.shared_back.at[z], ns.shared_back.at[z], (b, flip(z, j)))
    ns.bias_sums[4:5, 0:ns.mid] = jnp.sum(squeezed_grad, axis=0, keepdims=True)
    ns.bias_sums[5:6, :] = jnp.sum(excited_grad, axis=0, keepdims=True)
    ns.bias_sums[6:7, :] = jnp.full((1, ns.width), jnp.sum(gate * along), F32)
    combined = jnp.concatenate(
        [value.astype(F32)[0:4] for value in (excited_low, hidden, squeezed_low, pooled)], axis=1)
    quarter = combined.shape[1] // 4
    ns.factor_slots[z] = jnp.concatenate(
        [combined[:, q * quarter:(q + 1) * quarter] for q in range(4)], axis=0).astype(BF)
    ns.factors.along_row()


def take_gates(ns):
    ns.back.arrived(0, 1, 2)
    half = ns.width // 2
    for r in range(4):
        value = ns.shared_back[r].astype(F32)
        for k in range(4):
            ns.gates[k // 2, 4 * r:4 * r + 4, (k % 2) * half:(k % 2 + 1) * half] = value[4 * k:4 * k + 4]


def branch_back(ns):
    ns.widen_sum[...] = jnp.zeros_like(ns.widen_sum)

    def body(i, carry):
        rows = tile(i, 32)
        gate, pooled_grad = ns.gates[0, pl.ds(i, 1), :], ns.gates[1, pl.ds(i, 1), :]
        upstream = ns.cotangent[rows, :].astype(F32)
        strong = (alpha_res * ns.skip) * gate
        grad = upstream * strong + pooled_grad
        ns.out[rows, :] = (ns.images[rows, :].astype(F32) + strong * ns.out[rows, :].astype(F32)).astype(BF)
        ns.dx[rows, :] = grad.astype(BF)
        ns.widen_sum[...] += jnp.sum(grad.reshape(4, 8, ns.width), axis=0)
        return carry

    lax.fori_loop(0, ns.images.shape[0] // 32, body, 0)
    ns.bias_sums[3:4, :] = jnp.sum(ns.widen_sum[...], axis=0, keepdims=True)


def widen_grad(ns):
    def body(n, carry):
        lanes = tile(n, 256)
        ns.g[3][lanes, :] = dot(ns.dx[:, lanes], ns.act3[...], TN).astype(BF)
        return carry

    lax.fori_loop(0, ns.width // 256, body, 0)


def widen_back(ns, part):
    rows = tile(part, ns.strip)
    images = pl.ds(part * ns.blocks, ns.blocks)

    def body(n, carry):
        lanes = tile(n, 256)
        grad = dot(ns.dx[rows, :], ns.w[3][:, lanes], NN) * ns.slope2[rows, lanes].astype(F32)
        ns.bias_sums[2:3, lanes] += jnp.sum(grad, axis=0, keepdims=True)
        ns.low2[images, 16:48, lanes] = grad.reshape(ns.blocks, 32, 256).astype(BF)
        return carry

    lax.fori_loop(0, ns.mid // 256, body, 0)


def group_grad(ns, low, which):
    total = ns.images.shape[0]

    def body(g, carry):
        lanes = tile(g, GW)
        delta = low[:, 16:48, lanes].reshape(total, GW)
        ns.g[which][lanes, :] = dot(delta, ns.cols[g], TN).astype(BF)
        return carry

    lax.fori_loop(0, ns.mid // GW, body, 0)


def group_back(ns, part, which, slope_ref, target):
    rows = tile(part, ns.strip)
    images = pl.ds(part * ns.blocks, ns.blocks)

    def body(g, carry):
        lanes = tile(g, GW)
        stacked = jnp.concatenate(
            [ns.w[which][lanes, t * GW:(t + 1) * GW] for t in range(TAPS)], axis=0)
        grad = dot(ns.cols[g, rows, :], stacked, NN) * slope_ref[rows, lanes].astype(F32)
        ns.bias_sums[which - 1:which, lanes] += jnp.sum(grad, axis=0, keepdims=True)
        if target is ns.act3:
            target[rows, lanes] = grad.astype(BF)
        else:
            target[images, 16:48, lanes] = grad.reshape(ns.blocks, 32, GW).astype(BF)
        return carry

    lax.fori_loop(0, ns.mid // GW, body, 0)


def narrow_grad(ns):
    wide = ns.width // 512

    def body(k, carry):
        up, lanes = tile(k // wide, 256), tile(k % wide, 512)
        ns.g[0][up, lanes] = dot(ns.act3[:, up], ns.act0[:, lanes], TN).astype(BF)
        return carry

    lax.fori_loop(0, ns.mid // 256 * wide, body, 0)


def input_back(ns, part):
    rows = tile(part, ns.strip)

    def body(n, carry):
        lanes = tile(n, 256)
        grad = dot(ns.act3[rows, :], ns.w[0][:, lanes], NN)
        slope = gelu_pair(ns.images[rows, lanes].astype(F32), gamma_act * beta_in)[1]
        ns.dx[rows, lanes] = (ns.cotangent[rows, lanes].astype(F32) + grad * slope).astype(BF)
        return carry

    lax.fori_loop(0, ns.width // 256, body, 0)


def excite_grads(ns):
    b, z = place()
    device = b * 4 + z
    values = ns.factor_rows[...]
    at = [0, ns.width, ns.width + ns.mid, ns.width + 2 * ns.mid, 2 * ns.width + 2 * ns.mid]
    excited, hidden, squeezed, pooled = [values[:, at[k]:at[k + 1]] for k in range(4)]
    for own, other, share, target in (
        (excited, hidden, ns.shares[5], ns.grad_out[5]),
        (squeezed, pooled, ns.shares[4], ns.grad_out[4]),
    ):
        span = -(-share // 16) * 16
        wide = own.shape[1]
        lanes = lax.broadcasted_iota(jnp.int32, (span, wide), 1)
        ups = lax.broadcasted_iota(jnp.int32, (span, wide), 0)
        pick = jnp.where(lanes == ups + device * share, 1.0, 0.0).astype(BF)
        mine = dot(pick, own, NT).astype(BF)
        target[...] = dot(mine, other, NN)[:share]


def block_kernel(names, settings, *refs):
    ns = types.SimpleNamespace(**dict(zip(names, refs)), **settings)
    fits = ns.fits
    ns.strip = ns.images.shape[0] // ns.micro
    ns.blocks = ns.strip // 32
    ns.width = ns.images.shape[1]
    ns.w = [getattr(ns, f"w{k}") for k in range(6)]
    ns.g = [getattr(ns, f"g{k}", None) for k in range(4)]
    ns.mid = ns.w[0].shape[0]
    b, z = place()
    parts = range(ns.micro)
    fields = (ns.ext1, ns.ext2, ns.low2, ns.low1)
    for field in fields:
        edge = jnp.zeros((field.shape[0], 16, field.shape[2]), BF)
        field[:, 0:16, :] = edge
        field[:, 48:64, :] = edge
    ns.bias_sums[...] = jnp.zeros_like(ns.bias_sums)
    greet(fits)
    halo1, halo2, halo3, halo4 = [
        Halo(field, ns.halo_send.at[k], ns.halo_recv.at[k], ns.blocks) for k, field in enumerate(fields)]
    ns.pool = Transfer(ns.se_send.at[0], ns.se_recv.at[0])
    ns.back = Transfer(ns.se_send.at[1], ns.se_recv.at[1])
    ns.factors = Factors(
        ns.factor_slots, ns.factor_rows, ns.gather_send.at[7], ns.gather_recv.at[7], halves=False, block=16)
    jobs = []
    if fits:
        ns.gains = [column(ns.vecs[8 + k:9 + k, :], ns.shares[k]) for k in range(4)]
        ns.bias_slots[z] = ns.vecs[0:8, :]
        jobs.append(Gather(ns.bias_slots, ns.bias_rows, ns.gather_send.at[6], ns.gather_recv.at[6]))
        jobs[0].along_row()
        for k in range(6):
            slots, shard = getattr(ns, f"slots{k}"), getattr(ns, f"shard{k}")
            slots[z] = standard(shard, ns.gains[k]).astype(BF) if k < 4 else shard[...]
            jobs.append(Gather(slots, ns.w[k], ns.gather_send.at[k], ns.gather_recv.at[k]))
            jobs[-1].along_row()

    def pump(own=None, onward=None, corner=None, ready=None):
        if fits:
            if own is not None:
                jobs[own].own_block()
            if onward is not None:
                jobs[onward].onward()
            if corner is not None:
                jobs[corner].corner()
            if ready is not None:
                jobs[ready].ready()

    pump(own=0)
    pump(own=1)

    def first_act(i, carry):
        rows = tile(i, 32)
        ns.act0[rows, :] = (act_only(ns.images[rows, :].astype(F32)) * beta_in).astype(BF)
        return carry

    lax.fori_loop(0, ns.images.shape[0] // 32, first_act, 0)
    pump(onward=0, own=2)
    pump(onward=1, corner=0, own=3)
    pump(onward=2, corner=1, ready=0)
    if fits:
        for k in range(6):
            share = ns.shares[k]
            width = share * ns.devices
            ns.brow[k:k + 1, 0:width] = from_shares(ns.bias_rows[pl.ds(k, ns.devices, stride=8), :], share, width)
        ns.skip = ns.vecs[6:7, 0:1]
    else:
        ns.skip = ns.brow[6:7, 0:1]
    pump(ready=1)
    for part in parts:
        narrow_part(ns, part)
        halo1.start(part)
    pump(own=4, onward=3, corner=2, ready=2)
    for part in parts:
        halo1.arrived(part)
        build_columns(ns.ext1, ns.cols, ns.bucket, part, ns.blocks, False)
        group_part(ns, part, 1, ns.ext2, ns.slope1)
        halo2.start(part)
    pump(own=5, onward=4, corner=3, ready=3)
    for part in parts:
        halo2.arrived(part)
        build_columns(ns.ext2, ns.cols, ns.bucket, part, ns.blocks, False)
        group_part(ns, part, 2, ns.act3, ns.slope2)
    pump(own=6, onward=5, corner=4, ready=4)
    for part in parts:
        widen_part(ns, part)
    send_sums(ns)
    pump(onward=6, corner=5, ready=5)
    pump(corner=6, ready=6)
    excite_images(ns)
    for job in jobs:
        job.close()
    take_gates(ns)
    branch_back(ns)
    scatters = [None] * 5
    if fits:
        for k in range(5):
            refs_of = [getattr(ns, f"{name}{k}") for name in ("mate", "diagonal", "sides", "pieces", "landed")]
            scatters[k] = Scatter(
                ns.g[k] if k < 4 else ns.bias_parts, *refs_of, ns.scatter_send.at[k], ns.scatter_recv.at[k])

    def push(*steps):
        if fits:
            for name, k in steps:
                getattr(scatters[k], name)()

    widen_grad(ns)
    push(("to_mate", 3))
    for part in parts:
        widen_back(ns, part)
        halo3.start(part)
    push(("diagonals", 3))
    group_grad(ns, ns.low2, 2)
    push(("to_mate", 2), ("to_sides", 3))
    if fits:
        ns.factors.own_block()
    for part in parts:
        halo3.arrived(part)
        build_columns(ns.low2, ns.cols, ns.bucket, part, ns.blocks, True)
        group_back(ns, part, 2, ns.slope1, ns.low1)
        halo4.start(part)
    push(("diagonals", 2), ("along_row", 3))
    for part in parts:
        build_columns(ns.ext1, ns.cols, ns.bucket, part, ns.blocks, False)
    group_grad(ns, ns.low1, 1)
    push(("to_mate", 1), ("to_sides", 2))
    if fits:
        ns.factors.onward()
    for part in parts:
        halo4.arrived(part)
        build_columns(ns.low1, ns.cols, ns.bucket, part, ns.blocks, True)
        group_back(ns, part, 1, ns.slope0, ns.act3)
    push(("diagonals", 1))
    narrow_grad(ns)
    push(("to_mate", 0))
    if fits:
        for k in range(6):
            row = ns.bias_sums[k:k + 1, 0:ns.shares[k] * ns.devices]
            ns.bias_parts[pl.ds(k, ns.devices, stride=8), :] = to_shares(row, ns.devices, ns.shares[k])
        ns.bias_parts[pl.ds(6, ns.devices, stride=8), :] = jnp.broadcast_to(
            ns.bias_sums[6:7, 0:128], (ns.devices, 128))
        ns.bias_parts[pl.ds(7, ns.devices, stride=8), :] = jnp.zeros((ns.devices, 128), F32)
    push(("to_mate", 4), ("along_row", 2), ("to_sides", 1))
    for part in parts:
        input_back(ns, part)
        if part == 0:
            push(("diagonals", 0), ("diagonals", 4))
    push(("along_row", 1), ("to_sides", 0), ("to_sides", 4))
    if fits:
        ns.factors.corner()

        def settle(k):
            kernel_grad, gain_grad = standard_back(getattr(ns, f"shard{k}"), ns.gains[k], scatters[k].total())
            ns.grad_out[k][...] = kernel_grad
            ns.gain_out[k][...] = as_row(gain_grad, ns.shares[k])[:, 0:ns.shares[k]]

        for k in (3, 2):
            settle(k)
        ns.factors.ready()
        excite_grads(ns)
        push(("along_row", 0), ("along_row", 4))
        settle(1)
        settle(0)
        bias_total = scatters[4].total()
        for k in range(6):
            ns.bias_out[k][...] = bias_total[k:k + 1, 0:ns.shares[k]]
        ns.skip_out[...] = bias_total[6:7, 0:1]
        for job in scatters:
            job.close()
    else:
        ns.factor_out[...] = ns.factor_slots[z]
        ns.factors.arrived(0, 1, 2)
        ns.bias_sums_out[...] = ns.bias_sums[...]
    ns.factors.close()
    for halo in (halo1, halo2, halo3, halo4):
        for part in parts:
            halo.close(part)
    ns.pool.close()
    ns.back.close()


def run_block(images, bucket, cotangent, kernels, vectors, devices, fits):
    micro, blocks, strip, width = images.shape
    total = micro * blocks * strip
    mid = kernels[0].shape[0] * (devices if fits else 1)
    shares = [k.shape[0] // (1 if fits else devices) for k in kernels]
    vmem = pl.BlockSpec(memory_space=pltpu.VMEM)
    smem = pl.BlockSpec(memory_space=pltpu.SMEM)
    names, specs, args = [], [], []

    def operand(name, value, spec=vmem):
        names.append(name)
        specs.append(spec)
        args.append(value)

    operand("bucket", bucket, smem)
    operand("images", images.reshape(total, width))
    operand("cotangent", cotangent.reshape(total, width))
    for k, kernel in enumerate(kernels):
        operand(f"shard{k}" if fits else f"w{k}", kernel)
    operand("vecs" if fits else "brow", vectors)
    outs = []

    def result(name, shape, dtype):
        names.append(name)
        outs.append(jax.ShapeDtypeStruct(shape, dtype))

    result("out", (total, width), BF)
    result("dx", (total, width), BF)
    if fits:
        for k in range(6):
            result(f"grad_out{k}", kernels[k].shape, F32)
        for k in range(4):
            result(f"gain_out{k}", (1, shares[k]), F32)
        for k in range(6):
            result(f"bias_out{k}", (1, shares[k]), F32)
        result("skip_out", (1, 1), F32)
    else:
        for k in range(4):
            result(f"g{k}", kernels[k].shape, BF)
        result("factor_out", (16, (width + mid) // 2), BF)
        result("bias_sums_out", (8, width), F32)
    scratch = []

    def keep(name, shape, dtype):
        names.append(name)
        scratch.append(pltpu.VMEM(shape, dtype))

    images_here = micro * blocks
    whole_shapes = [(s * devices, k.shape[1]) for s, k in zip(shares, kernels)]
    if fits:
        for k, shape in enumerate(whole_shapes):
            keep(f"w{k}", shape, BF)
            keep(f"slots{k}", (4, shares[k], shape[1]), BF)
        keep("bias_slots", (4, 8, 128), F32)
        keep("bias_rows", (devices * 8, 128), F32)
        keep("brow", (8, width), F32)
        for k in (1, 2):
            keep(f"g{k}", whole_shapes[k], BF)
        keep("bias_parts", (devices * 8, 128), F32)
        for k in range(5):
            share, span, dtype = (shares[k], whole_shapes[k][1], BF) if k < 4 else (8, 128, F32)
            keep(f"mate{k}", (4, 4 * share, span), dtype)
            keep(f"diagonal{k}", (2, 2 * share, span), dtype)
            keep(f"sides{k}", (2, 4 * share, span), dtype)
            keep(f"pieces{k}", (4, share, span), dtype)
            keep(f"landed{k}", (3, share, span), dtype)
    keep("act0", (total, width), BF)
    for name in ("slope0", "slope1", "slope2", "act3"):
        keep(name, (total, mid), BF)
    for name in ("ext1", "ext2", "low2", "low1"):
        keep(name, (images_here, 64, mid), BF)
    keep("cols", (mid // GW, total, TAPS * GW), BF)
    keep("sums", (2, images_here, width), F32)
    keep("gates", (2, images_here, width), F32)
    keep("widen_sum", (8, width), F32)
    keep("bias_sums", (8, width), F32)
    keep("shared_out", (4, 16, width // 2), BF)
    keep("shared_in", (3, 16, width // 2), BF)
    keep("shared_back", (4, 16, width // 2), BF)
    keep("factor_slots", (4, 16, (width + mid) // 2), BF)
    keep("factor_rows", (devices // 4 * 16, 2 * (width + mid)), BF)
    for name, shape in (
        ("gather_send", (8, 11)), ("gather_recv", (8, 11)), ("scatter_send", (5, 11)), ("scatter_recv", (5, 11)),
        ("halo_send", (4, micro, 2)), ("halo_recv", (4, micro, 2)), ("se_send", (2, 3)), ("se_recv", (2, 3)),
    ):
        names.append(name)
        scratch.append(pltpu.SemaphoreType.DMA(shape))
    settings = dict(fits=fits, devices=devices, micro=micro, shares=shares)

    def kernel(*refs):
        by_name = dict(zip(names, refs))
        extra = {}
        if fits:
            extra["grad_out"] = [by_name[f"grad_out{k}"] for k in range(6)]
            extra["gain_out"] = [by_name[f"gain_out{k}"] for k in range(4)]
            extra["bias_out"] = [by_name[f"bias_out{k}"] for k in range(6)]
            extra["g0"], extra["g3"] = by_name["w4"], by_name["w5"]
        block_kernel(list(by_name) + list(extra), settings, *by_name.values(), *extra.values())

    return pl.pallas_call(
        kernel,
        out_shape=outs,
        in_specs=specs,
        out_specs=[vmem] * len(outs),
        scratch_shapes=scratch,
        compiler_params=pltpu.CompilerParams(
            collective_id=0, has_side_effects=True, vmem_limit_bytes=63 << 20),
    )(*args)


def scaled_std(kernel, gain):
    fan = kernel.shape[1]
    center = kernel - jnp.mean(kernel, axis=1, keepdims=True)
    spread = jnp.mean(jnp.square(center), axis=1, keepdims=True)
    return gain[:, None] * center * lax.rsqrt(fan * spread + eps_std)


def padded(vector):
    return jnp.pad(vector.astype(F32), (0, 128 - vector.shape[0]))


def body(
    images, bucket, cotangent,
    narrow_kernel, narrow_gain, narrow_bias, first_kernel, first_gain, first_bias,
    second_kernel, second_gain, second_bias, widen_kernel, widen_gain, widen_bias,
    squeeze_kernel, squeeze_bias, excite_kernel, excite_bias, skip_gain,
):
    axes = ("batch", "row")
    devices = lax.axis_size(axes)
    fits = lax.axis_size("batch") == 8
    shape = images.shape
    kernels = [narrow_kernel, first_kernel, second_kernel, widen_kernel]
    maps = [squeeze_kernel, excite_kernel]
    gains = [narrow_gain, first_gain, second_gain, widen_gain]
    biases = [narrow_bias, first_bias, second_bias, widen_bias, squeeze_bias, excite_bias]
    if fits:
        none = jnp.zeros((1,), F32)
        rows = biases + [skip_gain, none] + gains + [none] * 4
        vectors = jnp.stack([padded(row) for row in rows])
        got = run_block(images, bucket, cotangent, kernels + maps, vectors, devices, True)
        output, input_grad = got[0], got[1]
        kernel_grads, gain_grads = got[2:8], [g.reshape(-1) for g in got[8:12]]
        bias_grads, skip_grad = [g.reshape(-1) for g in got[12:18]], got[18].reshape(1)
    else:
        gather = functools.partial(lax.all_gather, axis_name=axes, axis=0, tiled=True)
        scatter = functools.partial(lax.psum_scatter, axis_name=axes, scatter_dimension=0, tiled=True)
        floats = [(k.astype(F32), g.astype(F32)) for k, g in zip(kernels, gains)]
        wholes = [gather(scaled_std(k, g).astype(BF)) for k, g in floats] + [gather(m) for m in maps]
        width = shape[3]
        rows = [gather(bias).astype(F32) for bias in biases] + [skip_gain.astype(F32), jnp.zeros((1,), F32)]
        vectors = jnp.stack([jnp.pad(row, (0, width - row.shape[0])) for row in rows])
        got = run_block(images, bucket, cotangent, wholes, vectors, devices, False)
        output, input_grad = got[0], got[1]
        totals = [scatter(g.astype(F32)) for g in got[2:6]]
        pulled = [jax.vjp(scaled_std, k, g)[1](t) for (k, g), t in zip(floats, totals)]
        kernel_grads, gain_grads = [p[0] for p in pulled], [p[1] for p in pulled]
        sums = got[7]
        bias_grads = [scatter(sums[k, :wholes[k].shape[0]]) for k in range(6)]
        skip_grad = lax.psum(sums[6, 0:1], axes)
        mid = wholes[0].shape[0]
        packed = gather(got[6]).reshape(devices, 4, 4, -1)
        values = jnp.transpose(packed, (0, 2, 1, 3)).reshape(devices * 4, -1)
        excited, hidden, squeezed, pooled = jnp.split(values, [width, width + mid, width + 2 * mid], axis=1)
        device = lax.axis_index(axes)
        for own, other, kernel in ((squeezed, pooled, squeeze_kernel), (excited, hidden, excite_kernel)):
            share = kernel.shape[0]
            mine = lax.dynamic_slice_in_dim(own, device * share, share, axis=1)
            kernel_grads.append(dot(mine, other, TN))
    return (
        output.reshape(shape), input_grad.reshape(shape),
        kernel_grads[0], gain_grads[0], bias_grads[0],
        kernel_grads[1], gain_grads[1], bias_grads[1],
        kernel_grads[2], gain_grads[2], bias_grads[2],
        kernel_grads[3], gain_grads[3], bias_grads[3],
        kernel_grads[4], bias_grads[4], kernel_grads[5], bias_grads[5],
        skip_grad,
    )


def solution(mesh):
    maps, shared = P(None, "batch", "row", None), P(("batch", "row"))
    rows = P(("batch", "row"), None)
    weight = (rows, shared, shared)
    return jax.shard_map(
        body,
        mesh=mesh,
        in_specs=(maps, P(None, "batch"), maps, *weight * 4, rows, shared, rows, shared, P()),
        out_specs=(maps, maps, *weight * 4, rows, shared, rows, shared, P()),
        check_vma=False,
    )
```

time: 1110 us -> 176 us (0.16)
  waiting for transfers between devices: 399 us -> 0 us
  local copies, waits for them, and re-layouts: 353 us -> 14.3 us
  Pallas kernels: 0 us -> 155 us
  other arithmetic: 110 us -> 4.02 us
  matrix products: 87 us -> 0 us
  blocking collectives: 84.8 us -> 0 us
  starting transfers between devices: 46.8 us -> 0 us
  between operations: 19.2 us -> 3.21 us
    reduce_scatter x4 -> x0, waiting for transfers between devices: 311 us -> none  [the longest x1 112 us: body(): lax.psum_scatter(grads[4], ('batch', 'row'), scatter_dimension=0, tiled=T...]
    pallas_call x0 -> x1, Pallas kernels: none -> 155 us  [run_block(): pl.pallas_call(kernel, out_shape=outs, in_specs=specs, out_specs=[vmem] *...]
    another operation x80 -> x2, local copies, waits for them, and re-layouts: 148 us -> 1.22 us  [body(): vectors = jnp.stack([padded(row) for row in rows])]
    dot_general x36 -> x0, matrix products: 87 us -> none  [the longest x8 33.3 us: spread(): jnp.einsum('rgk,gok->rgo', cols, shaped, preferred_element_type=jnp.float32)]
    unnamed x2 -> x0, blocking collectives: 84.8 us -> none
    reshape x18 -> x0, local copies, waits for them, and re-layouts: 80 us -> none  [the longest x8 61.4 us: columns(): return stacked.reshape(blocks * strip, groups, 9 * GW)]
    unnamed x485 -> x52, local copies, waits for them, and re-layouts: 74.8 us -> 13.1 us
    all_gather x6 -> x0, waiting for transfers between devices: 58 us -> none  [the longest x1 57.9 us: body(): lax.all_gather(excite_kernel, ('batch', 'row'), axis=0, tiled=True)]
  transfers between devices with their start and end apart: 29 -> 0, of which waited for: 8 -> 0; matrix products, arithmetic and copies ran while one was open for 45% -> 0% of each run, Pallas kernels for 0% -> 0%
where the time goes in v1:
time: 176 us
  Pallas kernels  155 us (88%)
  local copies, waits for them, and re-layouts  14.3 us (8%)
  other arithmetic  4.02 us (2%)
  between operations  3.21 us (2%)
    pallas_call x1, Pallas kernels, run_block(): pl.pallas_call(kernel, out_shape=outs, in_specs=specs, out_specs=[vmem] *...  155 us
    unnamed x52, local copies, waits for them, and re-layouts  13.1 us
    another operation x6, other arithmetic, body(): vectors = jnp.stack([padded(row) for row in rows])  4.02 us

profile of v1, /device:TPU:0, one launch (start us, length us, event | category | flops | bytes accessed | tf_op | source)
XLA Modules:
  0.0 176.1 jit_solution(13016213370119342115)
XLA Ops:
  1.3 0.7 bitcast_convert_fusion.10
  2.0 0.7 bitcast_convert_fusion.4
  2.6 0.7 bitcast_convert_fusion.2
  3.3 0.7 bitcast_convert_fusion.8
  4.0 0.7 bitcast_convert_fusion
  4.7 0.7 bitcast_convert_fusion.6
  5.3 1.2 stack.99.refs_9_
  6.6 154.5 %shard_map.339 = (bf16[512,1536]{1,0:T(8,128)(2,1)}, bf16[512,1536]{1,0:T(8,128)(2,1)}, f32[24,1536]{1,0:T(8,128)}, f32[24,1152]{1,0:T(8,128)}, f32[24,1152]{1,0...) custom-call(s32[2,8]{1,0:T(2,128)} %refs_0_.1, ...), custom_call_target="tpu_custom_call" | custom-call | tf_op jit(solution)/shard_map/pallas_call | solution.py:856
  161.1 0.0 copy-start
  161.1 2.8 %copy.59 = bf16[2,8,32,1536]{3,2,1,0:T(8,128)(2,1)} copy(bf16[2,8,32,1536]{3,2,1,0:T(8,128)(2,1)} %bitcast.51) | data formatting | bytes 3145728
  163.9 0.0 copy-done
  163.9 0.0 copy-start.4
  163.9 0.0 copy-start.16
  163.9 0.0 copy-start.15
  163.9 0.0 copy-start.6
  163.9 0.0 copy-start.14
  163.9 0.0 copy-start.13
  164.0 0.0 copy-start.5
  164.0 0.0 copy-start.12
  164.0 0.0 copy-start.11
  164.0 0.0 copy-start.3
  164.0 0.0 copy-start.10
  164.0 0.0 copy-start.9
  164.0 0.0 copy-start.2
  164.0 0.0 copy-start.8
  164.0 0.0 copy-start.1
  164.0 1.1 copy.60
  165.2 0.0 copy-done.4
  165.2 0.0 copy-start.7
  165.2 0.7 copy.61
  165.9 0.0 copy-done.16
  165.9 0.5 copy.62
  166.4 0.0 copy-done.15
  166.4 0.5 copy.63
  166.9 0.0 copy-done.6
  166.9 0.6 copy.64
  167.5 0.0 copy-done.14
  167.5 0.5 copy.65
  168.1 0.0 copy-done.13
  168.1 0.5 copy.66
  168.6 0.0 copy-done.5
  168.6 0.6 copy.67
  169.2 0.0 copy-done.12
  169.2 0.5 copy.68
  169.7 0.0 copy-done.11
  169.7 0.5 copy.69
  170.2 0.0 copy-done.3
  170.2 0.7 copy.70
  170.9 0.0 copy-done.10
  170.9 0.5 copy.71
  171.4 0.0 copy-done.9
  171.4 0.5 copy.72
  171.9 0.0 copy-done.2
  171.9 0.7 copy.73
  172.6 0.0 copy-done.8
  172.6 0.5 copy.74
  173.1 0.0 copy-done.1
  173.1 0.7 copy.75
  173.8 0.0 copy-done.7
  173.8 0.5 copy.76
  (1 shorter events, 0.0 us)
Async XLA Ops:
  161.1 2.8 %copy-start = (bf16[512,1536]{1,0:T(8,128)(2,1)S(1)}, bf16[512,1536]{1,0:T(8,128)(2,1)}, u32[]{:S(2)}) copy-start(bf16[512,1536]{1,0:T(8,128)(2,1)} %get-tuple-element.39) | copy-start | bytes 4718596
  163.9 1.3 copy-start.4
  163.9 1.9 %copy-start.16 = (f32[1,24]{1,0:T(1,128)S(1)}, f32[1,24]{1,0:T(1,128)}, u32[]{:S(2)}) copy-start(f32[1,24]{1,0:T(1,128)} %get-tuple-element.41) | copy-start | bytes 292
  163.9 2.5 %copy-start.15 = (f32[1,24]{1,0:T(1,128)S(1)}, f32[1,24]{1,0:T(1,128)}, u32[]{:S(2)}) copy-start(f32[1,24]{1,0:T(1,128)} %get-tuple-element.42) | copy-start | bytes 292
  163.9 3.0 %copy-start.6 = (f32[24,1152]{1,0:T(8,128)S(1)}, f32[24,1152]{1,0:T(8,128)}, u32[]{:S(2)}) copy-start(f32[24,1152]{1,0:T(8,128)} %get-tuple-element.91) | copy-start | bytes 331780
  163.9 3.6 %copy-start.14 = (f32[1,24]{1,0:T(1,128)S(1)}, f32[1,24]{1,0:T(1,128)}, u32[]{:S(2)}) copy-start(f32[1,24]{1,0:T(1,128)} %get-tuple-element.44) | copy-start | bytes 292
  163.9 4.1 %copy-start.13 = (f32[1,24]{1,0:T(1,128)S(1)}, f32[1,24]{1,0:T(1,128)}, u32[]{:S(2)}) copy-start(f32[1,24]{1,0:T(1,128)} %get-tuple-element.45) | copy-start | bytes 292
  164.0 4.6 %copy-start.5 = (f32[24,1152]{1,0:T(8,128)S(1)}, f32[24,1152]{1,0:T(8,128)}, u32[]{:S(2)}) copy-start(f32[24,1152]{1,0:T(8,128)} %get-tuple-element.94) | copy-start | bytes 331780
  164.0 5.2 %copy-start.12 = (f32[1,24]{1,0:T(1,128)S(1)}, f32[1,24]{1,0:T(1,128)}, u32[]{:S(2)}) copy-start(f32[1,24]{1,0:T(1,128)} %get-tuple-element.47) | copy-start | bytes 292
  164.0 5.8 %copy-start.11 = (f32[1,24]{1,0:T(1,128)S(1)}, f32[1,24]{1,0:T(1,128)}, u32[]{:S(2)}) copy-start(f32[1,24]{1,0:T(1,128)} %get-tuple-element.48) | copy-start | bytes 292
  164.0 6.3 %copy-start.3 = (f32[48,768]{1,0:T(8,128)S(1)}, f32[48,768]{1,0:T(8,128)}, u32[]{:S(2)}) copy-start(f32[48,768]{1,0:T(8,128)} %get-tuple-element.97) | copy-start | bytes 442372
  164.0 6.9 %copy-start.10 = (f32[1,48]{1,0:T(1,128)S(1)}, f32[1,48]{1,0:T(1,128)}, u32[]{:S(2)}) copy-start(f32[1,48]{1,0:T(1,128)} %get-tuple-element.50) | copy-start | bytes 580
  164.0 7.4 %copy-start.9 = (f32[1,48]{1,0:T(1,128)S(1)}, f32[1,48]{1,0:T(1,128)}, u32[]{:S(2)}) copy-start(f32[1,48]{1,0:T(1,128)} %get-tuple-element.51) | copy-start | bytes 580
  164.0 7.9 %copy-start.2 = (f32[24,1536]{1,0:T(8,128)S(1)}, f32[24,1536]{1,0:T(8,128)}, u32[]{:S(2)}) copy-start(f32[24,1536]{1,0:T(8,128)} %get-tuple-element.100) | copy-start | bytes 442372
  164.0 8.6 %copy-start.8 = (f32[1,24]{1,0:T(1,128)S(1)}, f32[1,24]{1,0:T(1,128)}, u32[]{:S(2)}) copy-start(f32[1,24]{1,0:T(1,128)} %get-tuple-element.53) | copy-start | bytes 292
  164.0 9.1 %copy-start.1 = (f32[48,768]{1,0:T(8,128)S(1)}, f32[48,768]{1,0:T(8,128)}, u32[]{:S(2)}) copy-start(f32[48,768]{1,0:T(8,128)} %get-tuple-element.102) | copy-start | bytes 442372
  165.2 8.6 %copy-start.7 = (f32[1,48]{1,0:T(1,128)S(1)}, f32[1,48]{1,0:T(1,128)}, u32[]{:S(2)}) copy-start(f32[1,48]{1,0:T(1,128)} %get-tuple-element.55) | copy-start | bytes 580

commit v2 on v1

v2 whole, which is shorter than its diff:
```python
import functools
import math
import types

import jax
import jax.numpy as jnp
from jax import lax
from jax.experimental import pallas as pl
from jax.experimental.pallas import tpu as pltpu
from jax.sharding import PartitionSpec as P

MESH = pl.DeviceIdType.MESH
BF = jnp.bfloat16
F32 = jnp.float32

GW = 128
PIX = 128
TAPS = 9
gamma_act = 1.7015
alpha_res = 0.2
beta_in = 0.9622504486493763
eps_std = 0.0001
tanh_scale = math.sqrt(2.0 / math.pi)
tanh_cube = 0.044715

NN = ((1,), (0,))
NT = ((1,), (1,))
TN = ((0,), (0,))


def dot(left, right, dims):
    return lax.dot_general(left, right, (dims, ((), ())), preferred_element_type=F32)


def place():
    return lax.axis_index("batch"), lax.axis_index("row")


def flip(value, bit):
    return lax.bitwise_xor(value, jnp.int32(bit))


def tile(index, size):
    return pl.ds(pl.multiple_of(index * size, size), size)


def greet(everywhere):
    b, z = place()
    barrier = pltpu.get_barrier_semaphore()
    for bit in (1, 2, 3):
        pl.semaphore_signal(barrier, inc=1, device_id=(b, flip(z, bit)), device_id_type=MESH)
    if everywhere:
        for bit in (1, 2, 4):
            pl.semaphore_signal(barrier, inc=1, device_id=(flip(b, bit), z), device_id_type=MESH)
    pl.semaphore_wait(barrier, 6 if everywhere else 3)


class Transfer:
    def __init__(self, send, recv):
        self.send, self.recv, self.copies = send, recv, {}

    def copy(self, key, src, dst, device):
        made = pltpu.make_async_remote_copy(
            src_ref=src, dst_ref=dst, send_sem=self.send.at[key], recv_sem=self.recv.at[key],
            device_id=device, device_id_type=MESH)
        made.start()
        self.copies[key] = made

    def arrived(self, *keys):
        for key in keys:
            self.copies[key].wait_recv()

    def close(self):
        for made in self.copies.values():
            made.wait_send()


class Gather(Transfer):
    def __init__(self, slots, whole, send, recv):
        super().__init__(send, recv)
        self.slots, self.whole = slots, whole
        self.rows = slots.shape[1]
        self.block = 4 * self.rows
        self.half = self.block // 2

    def at(self, index, start=0, size=None):
        size = self.block if size is None else size
        return self.whole.at[pl.ds(pl.multiple_of(index * self.block + start, 8 if self.rows == 8 else 16), size)]

    def along_row(self):
        b, z = place()
        for j in (1, 2, 3):
            self.copy(j - 1, self.slots.at[z], self.slots.at[z], (b, flip(z, j)))

    def assemble(self):
        b, z = place()
        base = pl.multiple_of(b * self.block, 16)
        if self.rows % 16 == 0:
            for r in range(4):
                self.whole[pl.ds(base + r * self.rows, self.rows)] = self.slots[r]
        else:
            for r in (0, 2):
                pair = jnp.concatenate([self.slots[r].astype(F32), self.slots[r + 1].astype(F32)], axis=0)
                self.whole[pl.ds(base + r * self.rows, 2 * self.rows)] = pair.astype(self.whole.dtype)

    def own_block(self):
        b, z = place()
        self.arrived(0, 1, 2)
        self.assemble()
        own = self.at(b)
        self.copy(3, own, own, (flip(b, 2), z))
        self.copy(4, own, own, (flip(b, 4), z))
        self.copy(5, own, own, (flip(b, 1), z))

    def onward(self):
        b, z = place()
        self.arrived(3)
        low = self.at(flip(b, 2), 0, self.half)
        self.copy(6, low, low, (flip(b, 4), z))
        near = self.at(flip(b, 2))
        self.copy(8, near, near, (flip(b, 1), z))
        self.arrived(4)
        high = self.at(flip(b, 4), self.half, self.half)
        self.copy(7, high, high, (flip(b, 2), z))
        near = self.at(flip(b, 4))
        self.copy(9, near, near, (flip(b, 1), z))

    def corner(self):
        b, z = place()
        self.arrived(6, 7)
        far = self.at(flip(b, 6))
        self.copy(10, far, far, (flip(b, 1), z))

    def ready(self):
        self.arrived(5, 8, 9, 10)


class PlaneGather(Transfer):
    def __init__(self, whole, send, recv, bit):
        super().__init__(send, recv)
        self.whole, self.bit = whole, bit

    def copy_block(self, key, index, bit):
        b, z = place()
        block = self.whole.at[index]
        self.copy(key, block, block, (flip(b, bit), z))

    def own_block(self):
        b, z = place()
        for key, bit in ((0, 2), (1, 4), (2, 1)):
            self.copy_block(key, b, bit)

    def onward(self):
        b, z = place()
        for key, bit in ((0, 2), (1, 4)):
            self.arrived(key)
            if self.bit != bit:
                self.copy_block(6, flip(b, bit), self.bit)
            self.copy_block(3 + key, flip(b, bit), 1)

    def corner(self):
        b, z = place()
        self.arrived(6)
        self.copy_block(5, flip(b, 6), 1)

    def ready(self):
        self.arrived(2, 3, 4, 5)


class Scatter(Transfer):
    def __init__(self, whole, mate, diagonal, sides, pieces, landed, send, recv):
        super().__init__(send, recv)
        self.whole, self.mate, self.diagonal, self.sides = whole, mate, diagonal, sides
        self.pieces, self.landed = pieces, landed
        self.rows = pieces.shape[1]
        self.block = 4 * self.rows
        self.half = self.block // 2

    def at(self, index, start=0, size=None):
        size = self.block if size is None else size
        return self.whole.at[pl.ds(pl.multiple_of(index * self.block + start, 16), size)]

    def to_mate(self):
        b, z = place()
        for k, q in enumerate((6, 2, 4, 0)):
            self.copy(k, self.at(flip(b, 1 ^ q)), self.mate.at[k], (flip(b, 1), z))

    def add(self, index, start, size, ref):
        where = pl.ds(pl.multiple_of(index * self.block + start, 16), size)
        total = self.whole[where].astype(F32) + ref[...].astype(F32)
        self.whole[where] = total.astype(self.whole.dtype)

    def diagonals(self):
        b, z = place()
        x_mate, y_mate = (flip(b, 2), z), (flip(b, 4), z)
        low, high = pl.ds(0, self.half), pl.ds(self.half, self.half)
        self.arrived(0)
        self.add(flip(b, 6), 0, self.block, self.mate.at[0])
        self.copy(4, self.at(flip(b, 6), 0, self.half), self.diagonal.at[0], y_mate)
        self.copy(5, self.at(flip(b, 6), self.half, self.half), self.diagonal.at[1], x_mate)
        self.arrived(1)
        self.add(flip(b, 2), 0, self.block, self.mate.at[1])
        self.copy(6, self.at(flip(b, 2), self.half, self.half), self.sides.at[0, high], x_mate)
        self.arrived(2)
        self.add(flip(b, 4), 0, self.block, self.mate.at[2])
        self.copy(7, self.at(flip(b, 4), 0, self.half), self.sides.at[1, low], y_mate)

    def to_sides(self):
        b, z = place()
        low, high = pl.ds(0, self.half), pl.ds(self.half, self.half)
        self.arrived(4)
        self.add(flip(b, 2), 0, self.half, self.diagonal.at[0])
        self.copy(8, self.at(flip(b, 2), 0, self.half), self.sides.at[0, low], (flip(b, 2), z))
        self.arrived(5)
        self.add(flip(b, 4), self.half, self.half, self.diagonal.at[1])
        self.copy(9, self.at(flip(b, 4), self.half, self.half), self.sides.at[1, high], (flip(b, 4), z))

    def along_row(self):
        b, z = place()
        self.arrived(3, 6, 7, 8, 9)
        step = 1 if self.rows % 16 == 0 else 2
        size = step * self.rows
        for r in range(0, 4, step):
            start = r * self.rows
            part = self.whole[pl.ds(pl.multiple_of(b * self.block + start, 16), size)].astype(F32)
            for held in (self.mate.at[3], self.sides.at[0], self.sides.at[1]):
                part += held[start:start + size].astype(F32)
            for k in range(step):
                self.pieces[r + k] = part[k * self.rows:(k + 1) * self.rows].astype(self.pieces.dtype)
        for j in (1, 2, 3):
            self.copy(9 + j, self.pieces.at[flip(z, j)], self.landed.at[j - 1], (b, flip(z, j)))

    def total(self):
        b, z = place()
        result = self.pieces[z].astype(F32)
        for j in (1, 2, 3):
            self.arrived(9 + j)
            result += self.landed[j - 1].astype(F32)
        return result


class Halo:
    def __init__(self, field, send, recv, blocks):
        self.field, self.send, self.recv, self.blocks = field, send, recv, blocks

    def made(self, part, way):
        b, z = place()
        images = pl.ds(part * self.blocks, self.blocks)
        source, target, step = ((32, 0, 1), (16, 48, -1))[way]
        return pltpu.make_async_remote_copy(
            src_ref=self.field.at[images, pl.ds(source, 16)], dst_ref=self.field.at[images, pl.ds(target, 16)],
            send_sem=self.send.at[part, way], recv_sem=self.recv.at[part, way],
            device_id=(b, z + step), device_id_type=MESH)

    def each(self, part, low, high, act):
        b, z = place()

        @pl.when(z < 3)
        def _():
            act(self.made(part, low))

        @pl.when(z > 0)
        def _():
            act(self.made(part, high))

    def clear_ends(self):
        b, z = place()
        edge = jnp.zeros((self.field.shape[0], 16, self.field.shape[2]), BF)

        @pl.when(z == 0)
        def _():
            self.field[:, 0:16, :] = edge

        @pl.when(z == 3)
        def _():
            self.field[:, 48:64, :] = edge

    def start(self, part):
        self.each(part, 0, 1, lambda made: made.start())

    def arrived(self, part):
        self.each(part, 1, 0, lambda made: made.wait_recv())

    def close(self, part):
        self.each(part, 0, 1, lambda made: made.wait_send())


def act_only(value):
    inner = jnp.tanh(tanh_scale * value * (1.0 + tanh_cube * (value * value)))
    return (0.5 * gamma_act) * value * (1.0 + inner)


def gelu_pair(value, scale):
    square = value * value
    inner = jnp.tanh(tanh_scale * value * (1.0 + tanh_cube * square))
    half = 0.5 + 0.5 * inner
    slope = half + (0.5 * tanh_scale) * value * (1.0 - inner * inner) * (1.0 + (3.0 * tanh_cube) * square)
    return scale * value * half, scale * slope


def column(row, count):
    lanes = lax.broadcasted_iota(jnp.int32, (count, 128), 1)
    ups = lax.broadcasted_iota(jnp.int32, (count, 128), 0)
    return jnp.sum(jnp.where(lanes == ups, row, 0.0), axis=1, keepdims=True)


def as_row(col, count):
    lanes = lax.broadcasted_iota(jnp.int32, (count, 128), 1)
    ups = lax.broadcasted_iota(jnp.int32, (count, 128), 0)
    return jnp.sum(jnp.where(lanes == ups, col, 0.0), axis=0, keepdims=True)


def centred(kernel_ref):
    kernel = kernel_ref[...].astype(F32)
    fan = kernel.shape[1]
    center = kernel - jnp.mean(kernel, axis=1, keepdims=True)
    spread = jnp.mean(center * center, axis=1, keepdims=True)
    return center, lax.rsqrt(fan * spread + eps_std)


def standard(kernel_ref, gain):
    center, scale = centred(kernel_ref)
    return gain * center * scale


def standard_back(kernel_ref, gain, cotan):
    center, scale = centred(kernel_ref)
    along = jnp.sum(cotan * center, axis=1, keepdims=True)
    mean = jnp.mean(cotan, axis=1, keepdims=True)
    kernel_grad = (gain * scale) * (cotan - mean) - (gain * along * scale * scale * scale) * center
    return kernel_grad, along * scale


def remainder(value, size):
    count = jnp.floor((value + 0.5) * (1.0 / size))
    return value - size * count, count


def owners(devices, share, width, row=None):
    index = lax.broadcasted_iota(jnp.int32, (128, width), 1).astype(F32)
    slot = lax.broadcasted_iota(jnp.int32, (128, width), 0).astype(F32)
    pick = jnp.where(remainder(index, share)[0] == slot, 1.0, 0.0).astype(BF)
    index = lax.broadcasted_iota(jnp.int32, (devices, width), 1)
    owner = lax.broadcasted_iota(jnp.int32, (devices, width), 0)
    start = owner * share if row is None else lax.shift_right_logical(owner, 2) * share
    mine = (index >= start) & (index < start + share)
    if row is not None:
        mine = mine & (jnp.bitwise_and(owner, 3) == row)
    return pick, mine


def from_shares(shares, share, width, row=None):
    pick, mine = owners(shares.shape[0], share, width, row)
    spread = dot(shares.astype(BF), pick, NN)
    return jnp.sum(jnp.where(mine, spread, 0.0), axis=0, keepdims=True)


def to_shares(vector, devices, share, row=None):
    pick, mine = owners(devices, share, vector.shape[1], row)
    masked = jnp.where(mine, vector, 0.0)
    upper = masked.astype(BF)
    lower = (masked - upper.astype(F32)).astype(BF)
    return dot(upper, pick, NT) + dot(lower, pick, NT)


def row_order(groups, share):
    total = 4 * groups * share
    within, row = remainder(lax.broadcasted_iota(jnp.int32, (total, 1), 0).astype(F32), groups * share)
    entry, group = remainder(within, share)
    target = (group * 4 + row) * share + entry
    index = lax.broadcasted_iota(jnp.int32, (total, total), 1).astype(F32)
    return jnp.where(index == target, 1.0, 0.0).astype(BF)


def build_columns(field, cols, bucket, part, blocks, reverse):
    width = field.shape[2]

    def body(i, carry):
        image = part * blocks + i
        value = field[image].astype(F32)
        size = jnp.where(bucket[part, i] == 0, 16, 8)
        place_in = jnp.bitwise_and(lax.broadcasted_iota(jnp.int32, (64, width), 0), size - 1)
        left = jnp.where(place_in != 0, pltpu.roll(value, 1, 0), 0.0)
        right = jnp.where(place_in != size - 1, pltpu.roll(value, 63, 0), 0.0)
        wide = jnp.full((32, width), size, jnp.int32) == 16
        for step_col, moved in ((-1, left), (0, value), (1, right)):
            for step_row in (-1, 0, 1):
                if step_row == 0:
                    tap = moved[16:48]
                elif step_row == -1:
                    tap = jnp.where(wide, moved[0:32], moved[8:40])
                else:
                    tap = jnp.where(wide, moved[32:64], moved[24:56])
                t = (step_row + 1) * 3 + step_col + 1
                t = 8 - t if reverse else t
                tap = tap.astype(BF)
                rows = pl.ds(pl.multiple_of(image * 32, 32), 32)
                for g in range(width // GW):
                    cols[g, rows, t * GW:(t + 1) * GW] = tap[:, g * GW:(g + 1) * GW]
        return carry

    lax.fori_loop(0, blocks, body, 0)


def split_dot(left, pieces):
    total, at = None, 0
    for piece in pieces:
        part = dot(left[:, at:at + piece.shape[1]], piece[...], NT)
        total, at = part if total is None else total + part, at + piece.shape[1]
    return total


def narrow_part(ns, part):
    rows = tile(part, ns.strip)
    images = pl.ds(part * ns.blocks, ns.blocks)

    def body(n, carry):
        lanes = tile(n, 256)
        value = split_dot(ns.act0.at[rows], [w.at[lanes] for w in ns.w[0]]) + ns.brow[0:1, lanes]
        act, slope = gelu_pair(value, gamma_act)
        ns.slope0[rows, lanes] = slope.astype(BF)
        ns.ext1[images, 16:48, lanes] = act.reshape(ns.blocks, 32, 256).astype(BF)
        return carry

    lax.fori_loop(0, ns.mid // 256, body, 0)


def group_part(ns, part, which, cols, target, slope_ref):
    rows = tile(part, ns.strip)
    images = pl.ds(part * ns.blocks, ns.blocks)

    def body(g, carry):
        lanes = tile(g, GW)
        value = dot(cols[g, rows, :], ns.w[which][0][lanes, :], NT) + ns.brow[which:which + 1, lanes]
        act, slope = gelu_pair(value, gamma_act)
        slope_ref[rows, lanes] = slope.astype(BF)
        low = act.astype(BF)
        if target is ns.act3:
            target[rows, lanes] = low
            ns.third_sums[tile(part, ns.blocks), lanes] = jnp.sum(
                low.astype(F32).reshape(ns.blocks, 32, GW), axis=1)
        else:
            target[images, 16:48, lanes] = low.reshape(ns.blocks, 32, GW)
        return carry

    lax.fori_loop(0, ns.mid // GW, body, 0)


def widen_part(ns, part):
    rows = tile(part, ns.strip)

    def body(n, carry):
        lanes = tile(n, 256)
        branch = split_dot(ns.act3.at[rows], [w.at[lanes] for w in ns.w[3]]) + ns.brow[3:4, lanes]
        ns.out[rows, lanes] = branch.astype(BF)
        upstream = ns.cotangent[rows, lanes].astype(F32)
        ns.along_sums[tile(part, ns.blocks), lanes] = jnp.sum(
            (branch * upstream).reshape(ns.blocks, 32, 256), axis=1)
        return carry

    lax.fori_loop(0, ns.width // 256, body, 0)


def to_row(ns, group, source, target):
    b, z = place()
    for j in (1, 2, 3):
        group.copy(j - 1, source(flip(z, j)), target(j - 1), (b, flip(z, j)))


def to_all(ns, group, slots):
    b, z = place()
    to_row(ns, group, lambda r: slots.at[z], lambda j: slots.at[z])


def row_pieces(ns, value):
    share = ns.shares[5]
    for r in range(4):
        pieces = [value[:, (4 * p + r) * share:(4 * p + r + 1) * share] for p in range(ns.devices // 4)]
        yield r, jnp.concatenate(pieces, axis=1)


def send_third(ns):
    b, z = place()
    ns.third_slots[z] = ns.third_sums[...].astype(BF)
    to_all(ns, ns.third, ns.third_slots)


def send_along(ns):
    for r, value in row_pieces(ns, ns.along_sums[...]):
        ns.along_out[r] = value.astype(BF)
    to_row(ns, ns.along, lambda r: ns.along_out.at[r], lambda j: ns.along_in.at[j])


def prepare_maps(ns):
    ns.order[...] = row_order(ns.devices // 4, ns.shares[4])
    half = ns.mid // 2
    if ns.fits:
        share = ns.shares[4]
        for side, whole in enumerate(ns.squeeze_halves):
            span = whole.shape[2]
            for p in range(0, ns.devices // 4, 2):
                pair = jnp.concatenate([whole[p].astype(F32), whole[p + 1].astype(F32)], axis=0).astype(BF)
                ns.squeeze[p * share:(p + 2) * share, side * span:(side + 1) * span] = pair
        sides = [whole[...].reshape(-1, half) for whole in ns.excite_halves]
    else:
        sides = [ns.excite_whole[:, side * half:(side + 1) * half] for side in (0, 1)]
    moved = sum(dot(value, ns.order[:, side * half:(side + 1) * half], NT) for side, value in enumerate(sides))
    ns.excite[...] = moved.astype(BF)


def total_of(slots):
    return sum(slots[r].astype(F32) for r in range(4))


def received(own, landed):
    b, z = place()
    return own[z].astype(F32) + sum(landed[j].astype(F32) for j in range(3))


def squeeze_images(ns):
    b, z = place()
    quarter, span = ns.squeeze.shape[0], ns.excite.shape[0]
    ns.third.arrived(0, 1, 2)
    third = total_of(ns.third_slots)
    upper = third.astype(BF)
    lower = (third - upper.astype(F32)).astype(BF)
    both = split_dot(jnp.concatenate([upper, lower], axis=0), ns.w[3])
    count = third.shape[0]
    pooled = ((both[:count] + both[count:]) * (1.0 / PIX) + ns.brow[3:4, :]).astype(BF)
    squeezed = dot(pooled, ns.squeeze[...], NT) + ns.brow[4:5, 0:quarter]
    hidden, slope = gelu_pair(squeezed, 1.0)
    ns.squeeze_slope[...] = slope
    ns.hidden_slots[z] = hidden.astype(BF)
    to_all(ns, ns.hidden, ns.hidden_slots)
    ns.factor_rows[b, :, ns.factor_at[2]:ns.factor_at[3]] = pooled
    ns.factor_rows[b, :, ns.factor_at[3]:ns.factor_at[4]] = upper


def excite_images(ns):
    b, z = place()
    span = ns.excite.shape[0]
    ns.hidden.arrived(0, 1, 2)
    hidden = jnp.concatenate([ns.hidden_slots[r].astype(F32) for r in range(4)], axis=1).astype(BF)
    ns.sigmoid[...] = jax.nn.sigmoid(dot(hidden, ns.excite[...], NT) + ns.brow[5:6, 0:span])
    ns.gate_slots[z] = (2.0 * ns.sigmoid[...]).astype(BF)
    to_all(ns, ns.gate, ns.gate_slots)
    ns.factor_rows[b, :, ns.factor_at[1]:ns.factor_at[2]] = dot(hidden, ns.order[...], NN).astype(BF)


def take_gates(ns):
    share = ns.shares[5]
    ns.gate.arrived(0, 1, 2)
    slots = [ns.gate_slots[r].astype(F32) for r in range(4)]
    pieces = [slots[r][:, p * share:(p + 1) * share] for p in range(ns.devices // 4) for r in range(4)]
    ns.gates[...] = jnp.concatenate(pieces, axis=1)


def excite_back(ns):
    b, z = place()
    quarter, span = ns.squeeze.shape[0], ns.excite.shape[0]
    ns.along.arrived(0, 1, 2)
    along = alpha_res * received(ns.along_out, ns.along_in)
    sigmoid = ns.sigmoid[...]
    gate = 2.0 * sigmoid
    excited_grad = (ns.skip * along) * (gate * (1.0 - sigmoid))
    excited_low = excited_grad.astype(BF)
    partial = dot(excited_low, ns.excite[...], NN)
    for r in range(4):
        ns.hidden_out[r] = partial[:, r * quarter:(r + 1) * quarter].astype(BF)
    to_row(ns, ns.hidden_back, lambda r: ns.hidden_out.at[r], lambda j: ns.hidden_in.at[j])
    ns.bias_sums[5:6, 0:span] = jnp.sum(excited_grad, axis=0, keepdims=True)
    ns.bias_sums[6:7, :] = jnp.full((1, ns.width), jnp.sum(gate * along), F32)
    ns.factor_rows[b, :, 0:span] = excited_low


def squeeze_back(ns):
    b, z = place()
    quarter = ns.squeeze.shape[0]
    ns.hidden_back.arrived(0, 1, 2)
    squeezed_grad = received(ns.hidden_out, ns.hidden_in) * ns.squeeze_slope[...]
    squeezed_low = squeezed_grad.astype(BF)
    pooled_grad = dot(squeezed_low, ns.squeeze[...], NN) * (1.0 / PIX)
    low = pooled_grad.astype(BF)
    ns.back_slots[z] = jnp.concatenate([dot(low, w[...], NN) for w in ns.w[3]], axis=1).astype(BF)
    to_all(ns, ns.back, ns.back_slots)
    for r, value in row_pieces(ns, pooled_grad):
        ns.pooled_out[r] = value.astype(BF)
    to_row(ns, ns.pooled_back, lambda r: ns.pooled_out.at[r], lambda j: ns.pooled_in.at[j])
    ns.pooled_sum[...] = PIX * jnp.sum(pooled_grad, axis=0, keepdims=True)
    ns.bias_sums[4:5, 0:quarter] = jnp.sum(squeezed_grad, axis=0, keepdims=True)
    ns.late_rows[b, :, ns.excite.shape[0]:] = squeezed_low


def take_pooled(ns):
    b, z = place()
    ns.pooled_back.arrived(0, 1, 2)
    ns.late_rows[b, :, 0:ns.excite.shape[0]] = received(ns.pooled_out, ns.pooled_in).astype(BF)


def branch_back(ns, part):
    def body(i, carry):
        image = part * ns.blocks + i
        rows = tile(image, 32)
        grad = ns.cotangent[rows, :].astype(F32) * ((alpha_res * ns.skip) * ns.gates[pl.ds(image, 1), :])
        ns.dx[rows, :] = grad.astype(BF)
        ns.widen_sum[...] += jnp.sum(grad.reshape(4, 8, ns.width), axis=0)
        return carry

    lax.fori_loop(0, ns.blocks, body, 0)


def add_branch(ns):
    def body(image, carry):
        rows = tile(image, 32)
        strong = (alpha_res * ns.skip) * ns.gates[pl.ds(image, 1), :]
        ns.out[rows, :] = (ns.images[rows, :].astype(F32) + strong * ns.out[rows, :].astype(F32)).astype(BF)
        return carry

    lax.fori_loop(0, ns.images.shape[0] // 32, body, 0)


def widen_grad(ns):
    def body(n, carry):
        lanes = tile(n, 256)
        ns.g[3][0][lanes, :] = dot(ns.dx[:, lanes], ns.act3[...], TN).astype(BF)
        return carry

    lax.fori_loop(0, ns.width // 256, body, 0)


def widen_back(ns, part):
    rows = tile(part, ns.strip)
    images = pl.ds(part * ns.blocks, ns.blocks)
    for piece, w in enumerate(ns.w[3]):
        span = min(256, w.shape[1])

        def body(n, carry):
            here = tile(n, span)
            lanes = pl.ds(pl.multiple_of(piece * w.shape[1] + n * span, span), span)
            grad = dot(ns.dx[rows, :], w[:, here], NN)
            ns.ext2[images, 16:48, lanes] = grad.reshape(ns.blocks, 32, span).astype(BF)
            return carry

        lax.fori_loop(0, w.shape[1] // span, body, 0)


def third_back(ns, part):
    def body(i, carry):
        image = part * ns.blocks + i
        rows = tile(image, 32)
        grad = ns.ext2[image, 16:48, :].astype(F32) + ns.third_pooled[pl.ds(image, 1), :]
        grad = grad * ns.slope2[rows, :].astype(F32)
        ns.ext2[image, 16:48, :] = grad.astype(BF)
        ns.second_sum[...] += jnp.sum(grad.reshape(4, 8, ns.mid), axis=0)
        return carry

    lax.fori_loop(0, ns.blocks, body, 0)


def group_grad(ns, low, cols, which):
    total = ns.images.shape[0]

    def body(g, carry):
        lanes = tile(g, GW)
        delta = low[:, 16:48, lanes].reshape(total, GW)
        ns.g[which][0][lanes, :] = dot(delta, cols[g], TN).astype(BF)
        return carry

    lax.fori_loop(0, ns.mid // GW, body, 0)


def group_back(ns, part, which, slope_ref, target):
    rows = tile(part, ns.strip)
    images = pl.ds(part * ns.blocks, ns.blocks)

    def body(g, carry):
        lanes = tile(g, GW)
        stacked = jnp.concatenate(
            [ns.w[which][0][lanes, t * GW:(t + 1) * GW] for t in range(TAPS)], axis=0)
        grad = dot(ns.cols[g, rows, :], stacked, NN) * slope_ref[rows, lanes].astype(F32)
        ns.bias_sums[which - 1:which, lanes] += jnp.sum(grad, axis=0, keepdims=True)
        if target is ns.act3:
            target[rows, lanes] = grad.astype(BF)
        else:
            target[images, 16:48, lanes] = grad.reshape(ns.blocks, 32, GW).astype(BF)
        return carry

    lax.fori_loop(0, ns.mid // GW, body, 0)


def narrow_grad(ns, piece):
    target = ns.g[0][piece]
    span = target.shape[1]

    def body(k, carry):
        up = tile(k, 256)
        target[up, :] = dot(ns.act3[:, up], ns.act0[:, piece * span:(piece + 1) * span], TN).astype(BF)
        return carry

    lax.fori_loop(0, ns.mid // 256, body, 0)


def input_back(ns, part):
    rows = tile(part, ns.strip)
    for piece, w in enumerate(ns.w[0]):
        span = w.shape[1]

        def body(n, carry):
            here = tile(n, 256)
            lanes = pl.ds(pl.multiple_of(piece * span + n * 256, 256), 256)
            grad = dot(ns.act3[rows, :], w[:, here], NN)
            slope = gelu_pair(ns.images[rows, lanes].astype(F32), gamma_act * beta_in)[1]
            ns.dx[rows, lanes] = (ns.cotangent[rows, lanes].astype(F32) + grad * slope).astype(BF)
            return carry

        lax.fori_loop(0, span // 256, body, 0)


def excite_grads(ns):
    b, z = place()
    values = ns.factor_rows[...].reshape(-1, ns.factor_rows.shape[2])
    excited, hidden, pooled, third = [
        values[:, start:stop] for start, stop in zip(ns.factor_at[:-1], ns.factor_at[1:])]
    late = ns.late_rows[...].reshape(-1, ns.late_rows.shape[2])
    pooled_grad, squeezed = late[:, :ns.excite.shape[0]], late[:, ns.excite.shape[0]:]
    results = []
    for own, other, share in (
        (excited, hidden, ns.shares[5]), (squeezed, pooled, ns.shares[4]), (pooled_grad, third, ns.shares[5]),
    ):
        height = -(-share // 16) * 16
        lanes = lax.broadcasted_iota(jnp.int32, (height, own.shape[1]), 1)
        ups = lax.broadcasted_iota(jnp.int32, (height, own.shape[1]), 0)
        pick = jnp.where(lanes == ups + b * share, 1.0, 0.0).astype(BF)
        mine = dot(pick, own, NT).astype(BF)
        results.append(dot(mine, other, NN)[:share])
    ns.grad_out[5][...], ns.grad_out[4][...] = results[:2]
    return results[2]


def block_kernel(names, settings, *refs):
    ns = types.SimpleNamespace(**dict(zip(names, refs)), **settings)
    fits = ns.fits
    ns.strip = ns.images.shape[0] // ns.micro
    ns.blocks = ns.strip // 32
    ns.width = ns.images.shape[1]
    ns.w = [[getattr(ns, f"w{k}_{i}") for i in range(PIECES[k])] for k in range(4)]
    ns.g = [[getattr(ns, f"g{k}_{i}") for i in range(GRAD_PIECES[k])] for k in range(4)]
    ns.mid = ns.w[0][0].shape[0]
    b, z = place()
    parts = range(ns.micro)
    fields = (ns.ext1, ns.ext2, ns.ext2, ns.ext1)
    loads = [
        pltpu.make_async_copy(source, target, ns.local_sem.at[k])
        for k, (source, target) in enumerate(((ns.images_in, ns.images), (ns.cotangent_in, ns.cotangent)))]
    for load in loads:
        load.start()
    greet(fits)
    halo1, halo2, halo3, halo4 = halos = [
        Halo(field, ns.halo_send.at[k], ns.halo_recv.at[k], ns.blocks) for k, field in enumerate(fields)]
    groups = [Transfer(ns.se_send.at[k], ns.se_recv.at[k]) for k in range(7)]
    ns.third, ns.along, ns.hidden, ns.hidden_back, ns.gate, ns.back, ns.pooled_back = groups
    jobs, wanted = [], {}
    planes = []
    if fits:
        ns.squeeze_halves, ns.excite_halves = [], []
        for k, name, halves in ((4, "squeeze", ns.squeeze_halves), (5, "excite", ns.excite_halves)):
            shard = getattr(ns, f"shard{k}")
            for side, bit in ((0, 4), (1, 2)):
                whole = getattr(ns, f"{name}_half{side}")
                span = whole.shape[2]
                whole[b] = shard[:, side * span:(side + 1) * span]
                halves.append(whole)
                i = len(planes)
                planes.append(PlaneGather(whole, ns.plane_send.at[i], ns.plane_recv.at[i], bit))
                planes[i].own_block()
        ns.gains = [column(ns.vecs[8 + k:9 + k, :], ns.shares[k]) for k in range(4)]
        ns.bias_slots[z] = ns.vecs[0:8, :]
        jobs.append(Gather(ns.bias_slots, ns.bias_rows, ns.gather_send.at[0], ns.gather_recv.at[0]))
        jobs[0].along_row()
        for k in range(4):
            value = standard(getattr(ns, f"shard{k}"), ns.gains[k]).astype(BF)
            wanted[k] = []
            for piece, whole in enumerate(ns.w[k]):
                i, span = len(jobs), whole.shape[1]
                slots = getattr(ns, f"slots{k}_{piece}")
                slots[z] = value[:, piece * span:(piece + 1) * span]
                wanted[k].append(i)
                jobs.append(Gather(slots, whole, ns.gather_send.at[i], ns.gather_recv.at[i]))
                jobs[i].along_row()
        factors = PlaneGather(ns.factor_rows, ns.plane_send.at[4], ns.plane_recv.at[4], 4)
        late = PlaneGather(ns.late_rows, ns.plane_send.at[5], ns.plane_recv.at[5], 2)

    def own(k):
        if fits:
            jobs[k].own_block()

    def onward(k):
        if fits:
            jobs[k].onward()

    def corner(k):
        if fits:
            jobs[k].corner()

    def weight(k):
        for i in wanted.get(k, ()):
            jobs[i].ready()

    ns.bias_sums[...] = jnp.zeros_like(ns.bias_sums)
    ns.widen_sum[...] = jnp.zeros_like(ns.widen_sum)
    ns.second_sum[...] = jnp.zeros_like(ns.second_sum)
    halo1.clear_ends()
    halo2.clear_ends()
    loads[0].wait()
    own(0)

    def first_act(i, carry):
        rows = tile(i, 32)
        ns.act0[rows, :] = (act_only(ns.images[rows, :].astype(F32)) * beta_in).astype(BF)
        return carry

    lax.fori_loop(0, ns.images.shape[0] // 32, first_act, 0)
    for job in planes:
        job.onward()
    own(1)
    onward(0)
    own(2)
    onward(1)
    corner(0)
    own(3)
    for job in planes:
        job.corner()
    onward(2)
    onward(3)
    own(4)
    for job in planes:
        job.ready()
    prepare_maps(ns)
    corner(1)
    corner(2)
    corner(3)
    if fits:
        jobs[0].ready()
        for k in range(6):
            share, row = ns.shares[k], None if k < 4 else z
            width = share * (ns.devices if k < 4 else ns.devices // 4)
            shares = ns.bias_rows[pl.ds(k, ns.devices, stride=8), :]
            ns.brow[k:k + 1, 0:width] = from_shares(shares, share, width, row)
        ns.skip = ns.vecs[6:7, 0:1]
    else:
        ns.skip = ns.brow[6:7, 0:1]
    weight(0)
    narrow_part(ns, 0)
    halo1.start(0)
    own(5)
    narrow_part(ns, 1)
    halo1.start(1)
    onward(4)
    own(6)
    onward(5)
    corner(4)
    weight(1)

    def first_part(part):
        halo1.arrived(part)
        build_columns(ns.ext1, ns.first_cols, ns.bucket, part, ns.blocks, False)
        group_part(ns, part, 1, ns.first_cols, ns.ext2, ns.slope1)
        halo2.start(part)

    def second_part(part):
        halo2.arrived(part)
        build_columns(ns.ext2, ns.cols, ns.bucket, part, ns.blocks, False)
        group_part(ns, part, 2, ns.cols, ns.act3, ns.slope2)

    first_part(0)
    first_part(1)
    onward(6)
    corner(5)
    weight(2)
    second_part(0)
    corner(6)
    second_part(1)
    send_third(ns)
    loads[1].wait()
    weight(3)
    scatters = []
    if fits:
        for k, piece in SCATTERS:
            name = len(scatters)
            refs_of = [getattr(ns, f"{kind}{name}") for kind in ("mate", "diagonal", "sides", "pieces", "landed")]
            whole = ns.bias_parts if k is None else ns.g[k][piece]
            scatters.append(Scatter(whole, *refs_of, ns.scatter_send.at[name], ns.scatter_recv.at[name]))

    def to_mate(k):
        if fits:
            scatters[k].to_mate()

    def diagonals(k):
        if fits:
            scatters[k].diagonals()

    def sides(k):
        if fits:
            scatters[k].to_sides()

    def along_row(k):
        if fits:
            scatters[k].along_row()

    for halo in (halo1, halo2):
        for part in parts:
            halo.close(part)
    widen_part(ns, 0)
    squeeze_images(ns)
    widen_part(ns, 1)
    send_along(ns)
    excite_images(ns)
    take_gates(ns)
    excite_back(ns)
    if fits:
        factors.own_block()
    for part in parts:
        branch_back(ns, part)
    widen_grad(ns)
    to_mate(0)
    squeeze_back(ns)
    if fits:
        factors.onward()
    for part in parts:
        widen_back(ns, part)
    diagonals(0)
    ns.back.arrived(0, 1, 2)
    ns.third_pooled[...] = total_of(ns.back_slots)
    stores = []

    def store(source, target, start, size):
        rows = pl.ds(start, size)
        stores.append(pltpu.make_async_copy(source.at[rows], target.at[rows], ns.local_sem.at[len(stores)]))
        stores[-1].start()

    def third_grad(part):
        third_back(ns, part)
        halo3.start(part)

    def second_grad():
        group_grad(ns, ns.ext2, ns.cols, 2)
        to_mate(1)

    def second_back(part):
        halo3.arrived(part)
        build_columns(ns.ext2, ns.cols, ns.bucket, part, ns.blocks, True)
        group_back(ns, part, 2, ns.slope1, ns.ext1)
        halo4.start(part)

    def first_grad():
        group_grad(ns, ns.ext1, ns.first_cols, 1)
        to_mate(2)

    def first_back(part):
        halo4.arrived(part)
        build_columns(ns.ext1, ns.cols, ns.bucket, part, ns.blocks, True)
        group_back(ns, part, 1, ns.slope0, ns.act3)

    def narrow_piece(i):
        narrow_grad(ns, i)
        to_mate(3 + i)

    def bias_parts():
        ns.bias_sums[2:3, 0:ns.mid] = jnp.sum(ns.second_sum[...], axis=0, keepdims=True)
        ns.bias_sums[3:4, :] = jnp.sum(ns.widen_sum[...], axis=0, keepdims=True) + ns.pooled_sum[...]
        if fits:
            for k in range(6):
                share, row = ns.shares[k], None if k < 4 else z
                vector = ns.bias_sums[k:k + 1, 0:share * (ns.devices if k < 4 else ns.devices // 4)]
                ns.bias_parts[pl.ds(k, ns.devices, stride=8), :] = to_shares(vector, ns.devices, share, row)
            ns.bias_parts[pl.ds(6, ns.devices, stride=8), :] = jnp.broadcast_to(
                ns.bias_sums[6:7, 0:128], (ns.devices, 128))
            ns.bias_parts[pl.ds(7, ns.devices, stride=8), :] = jnp.zeros((ns.devices, 128), F32)
            to_mate(6)

    def input_grad(part):
        input_back(ns, part)
        store(ns.dx, ns.dx_to, part * ns.strip, ns.strip)

    def output():
        add_branch(ns)
        store(ns.out, ns.out_to, 0, 2 * ns.strip)

    def settle(k, total):
        kernel_grad, gain_grad = standard_back(getattr(ns, f"shard{k}"), ns.gains[k], total)
        ns.grad_out[k][...] = kernel_grad
        ns.small_out[8 + k:9 + k, :] = as_row(gain_grad, ns.shares[k])

    def settle_widen():
        factors.ready()
        late.ready()
        settle(3, scatters[0].total() + excite_grads(ns))

    def settle_narrow():
        settle(0, jnp.concatenate([scatters[3 + i].total() for i in range(GRAD_PIECES[0])], axis=1))

    def settle_biases():
        ns.small_out[0:8, :] = scatters[6].total()

    third_grad(0)
    third_grad(1)
    take_pooled(ns)
    if fits:
        late.own_block()
        factors.corner()
    second_grad()
    sides(0)
    output()
    diagonals(1)
    second_back(0)
    if fits:
        late.onward()
    second_back(1)
    sides(1)
    first_grad()
    first_back(0)
    diagonals(2)
    first_back(1)
    along_row(0)
    narrow_piece(0)
    narrow_piece(1)
    sides(2)
    narrow_piece(2)
    diagonals(3)
    diagonals(4)
    diagonals(5)
    bias_parts()
    sides(3)
    input_grad(0)
    sides(4)
    diagonals(6)
    sides(5)
    along_row(1)
    input_grad(1)
    along_row(3)
    sides(6)
    along_row(4)
    along_row(2)
    if fits:
        late.corner()
    along_row(5)
    along_row(6)
    if fits:
        settle(2, scatters[1].total())
    if fits:
        settle(1, scatters[2].total())
    if fits:
        settle_widen()
    if fits:
        settle_biases()
    if fits:
        settle_narrow()
    if fits:
        for job in scatters + jobs + planes + [factors, late]:
            job.close()
    else:
        ns.factor_out[:, :ns.factor_at[-1]] = ns.factor_rows[b]
        ns.factor_out[:, ns.factor_at[-1]:] = ns.late_rows[b]
        ns.bias_sums_out[...] = ns.bias_sums[...]
    for halo in (halo3, halo4):
        for part in parts:
            halo.close(part)
    for group in groups:
        group.close()
    for made in stores:
        made.wait()


PIECES = (3, 1, 1, 1)
GRAD_PIECES = (3, 1, 1, 1)
SCATTERS = ((3, 0), (2, 0), (1, 0), (0, 0), (0, 1), (0, 2), (None, 0))


def hand_over(*refs):
    small, wholes, rest = refs[8], refs[:8], refs[9:]
    for source, target in zip(wholes[:2], rest[:2]):
        target[...] = source[...]

    @pl.when(pl.program_id(0) == 0)
    def _():
        for source, target in zip(wholes[2:], rest[2:8]):
            target[...] = source[...]
        for k, target in enumerate(rest[8:12]):
            target[...] = small[8 + k:9 + k, 0:target.shape[1]]
        for k, target in enumerate(rest[12:18]):
            target[...] = small[k:k + 1, 0:target.shape[1]]
        rest[18][...] = small[6:7, 0:1]


def own_results(got, shares):
    steps = 4
    large = pl.BlockSpec((got[0].shape[0] // steps, got[0].shape[1]), lambda i: (i, 0))
    row = [jax.ShapeDtypeStruct((1, share), F32) for share in shares]
    like = [jax.ShapeDtypeStruct(value.shape, value.dtype) for value in got[:8]]
    results = like + row[:4] + row + [jax.ShapeDtypeStruct((1, 1), F32)]

    def specs(values):
        return [large] * 2 + [pl.BlockSpec(value.shape, lambda i: (0, 0)) for value in values[2:]]

    return pl.pallas_call(
        hand_over, grid=(steps,), out_shape=results, in_specs=specs(got), out_specs=specs(results))(*got)


def run_block(images, bucket, cotangent, kernels, vectors, devices, fits):
    micro, blocks, strip, width = images.shape
    total = micro * blocks * strip
    mid = kernels[0].shape[0] * (devices if fits else 1)
    quarter = devices // 4
    shares = [k.shape[0] // (1 if fits else devices if i < 4 else quarter) for i, k in enumerate(kernels)]
    vmem = pl.BlockSpec(memory_space=pltpu.VMEM)
    smem = pl.BlockSpec(memory_space=pltpu.SMEM)
    anywhere = pl.BlockSpec(memory_space=pl.ANY)
    spans = [quarter * shares[5], mid, width, mid]
    factor_at = [sum(spans[:k]) for k in range(5)]
    late_width = quarter * (shares[5] + shares[4])
    names, specs, args = [], [], []

    def operand(name, value, spec=vmem):
        names.append(name)
        specs.append(spec)
        args.append(value)

    operand("bucket", bucket, smem)
    operand("images_in", images.reshape(total, width), anywhere)
    operand("cotangent_in", cotangent.reshape(total, width), anywhere)
    for k, kernel in enumerate(kernels):
        if fits:
            operand(f"shard{k}", kernel)
        elif k < 4:
            for i, piece in enumerate(jnp.split(kernel, PIECES[k], axis=1)):
                operand(f"w{k}_{i}", piece)
        else:
            operand(("squeeze", "excite_whole")[k - 4], kernel)
    operand("vecs" if fits else "brow", vectors)
    outs = []

    def result(name, shape, dtype):
        names.append(name)
        outs.append(jax.ShapeDtypeStruct(shape, dtype))

    result("out_to", (total, width), BF)
    result("dx_to", (total, width), BF)
    if fits:
        for k in range(6):
            result(f"grad_out{k}", kernels[k].shape, F32)
        result("small_out", (16, 128), F32)
    else:
        for k in range(4):
            for i in range(GRAD_PIECES[k]):
                result(f"g{k}_{i}", (kernels[k].shape[0], kernels[k].shape[1] // GRAD_PIECES[k]), BF)
        result("factor_out", (micro * blocks, factor_at[-1] + late_width), BF)
        result("bias_sums_out", (8, width), F32)
    scratch = []

    def keep(name, shape, dtype):
        names.append(name)
        scratch.append(pltpu.VMEM(shape, dtype))

    images_here = micro * blocks
    whole_shapes = [(s * devices, k.shape[1]) for s, k in zip(shares, kernels)]
    if fits:
        for k, shape in enumerate(whole_shapes[:4]):
            for i in range(PIECES[k]):
                keep(f"w{k}_{i}", (shape[0], shape[1] // PIECES[k]), BF)
                keep(f"slots{k}_{i}", (4, shares[k], shape[1] // PIECES[k]), BF)
        keep("bias_slots", (4, 8, 128), F32)
        keep("bias_rows", (devices * 8, 128), F32)
        keep("brow", (8, width), F32)
        for k in range(4):
            for i in range(GRAD_PIECES[k]):
                keep(f"g{k}_{i}", (whole_shapes[k][0], whole_shapes[k][1] // GRAD_PIECES[k]), BF)
        keep("squeeze", (quarter * shares[4], width), BF)
        for side in (0, 1):
            keep(f"squeeze_half{side}", (quarter, shares[4], width // 2), BF)
            keep(f"excite_half{side}", (quarter, shares[5], mid // 2), BF)
        keep("bias_parts", (devices * 8, 128), F32)
        for i, (k, piece) in enumerate(SCATTERS):
            share, span, dtype = (8, 128, F32) if k is None else (shares[k], whole_shapes[k][1] // GRAD_PIECES[k], BF)
            keep(f"mate{i}", (4, 4 * share, span), dtype)
            keep(f"diagonal{i}", (2, 2 * share, span), dtype)
            keep(f"sides{i}", (2, 4 * share, span), dtype)
            keep(f"pieces{i}", (4, share, span), dtype)
            keep(f"landed{i}", (3, share, span), dtype)
    for name in ("images", "cotangent", "out", "dx"):
        keep(name, (total, width), BF)
    keep("act0", (total, width), BF)
    for name in ("slope0", "slope1", "slope2", "act3"):
        keep(name, (total, mid), BF)
    for name in ("ext1", "ext2"):
        keep(name, (images_here, 64, mid), BF)
    for name in ("first_cols", "cols"):
        keep(name, (mid // GW, total, TAPS * GW), BF)
    keep("third_sums", (images_here, mid), F32)
    keep("third_pooled", (images_here, mid), F32)
    keep("third_slots", (4, images_here, mid), BF)
    keep("along_sums", (images_here, width), F32)
    keep("gates", (images_here, width), F32)
    keep("sigmoid", (images_here, quarter * shares[5]), F32)
    keep("squeeze_slope", (images_here, quarter * shares[4]), F32)
    keep("widen_sum", (8, width), F32)
    keep("second_sum", (8, mid), F32)
    keep("pooled_sum", (1, width), F32)
    keep("bias_sums", (8, width), F32)
    keep("order", (mid, mid), BF)
    keep("excite", (quarter * shares[5], mid), BF)
    keep("pooled_out", (4, images_here, quarter * shares[5]), BF)
    keep("pooled_in", (3, images_here, quarter * shares[5]), BF)
    keep("along_out", (4, images_here, quarter * shares[5]), BF)
    keep("along_in", (3, images_here, quarter * shares[5]), BF)
    keep("hidden_slots", (4, images_here, quarter * shares[4]), BF)
    keep("hidden_out", (4, images_here, quarter * shares[4]), BF)
    keep("hidden_in", (3, images_here, quarter * shares[4]), BF)
    keep("gate_slots", (4, images_here, quarter * shares[5]), BF)
    keep("back_slots", (4, images_here, mid), BF)
    keep("factor_rows", (quarter, images_here, factor_at[-1]), BF)
    keep("late_rows", (quarter, images_here, late_width), BF)
    for name, shape in (
        ("gather_send", (9, 11)), ("gather_recv", (9, 11)), ("scatter_send", (7, 13)), ("scatter_recv", (7, 13)),
        ("local_sem", (4,)),
        ("plane_send", (6, 7)), ("plane_recv", (6, 7)),
        ("halo_send", (4, micro, 2)), ("halo_recv", (4, micro, 2)), ("se_send", (7, 3)), ("se_recv", (7, 3)),
    ):
        names.append(name)
        scratch.append(pltpu.SemaphoreType.DMA(shape))
    settings = dict(fits=fits, devices=devices, micro=micro, shares=shares, factor_at=factor_at)

    def kernel(*refs):
        by_name = dict(zip(names, refs))
        extra = {}
        if fits:
            extra["grad_out"] = [by_name[f"grad_out{k}"] for k in range(6)]
        block_kernel(list(by_name) + list(extra), settings, *by_name.values(), *extra.values())

    return pl.pallas_call(
        kernel,
        out_shape=outs,
        in_specs=specs,
        out_specs=[anywhere] * 2 + [vmem] * (len(outs) - 2),
        scratch_shapes=scratch,
        compiler_params=pltpu.CompilerParams(
            collective_id=0, has_side_effects=True, vmem_limit_bytes=63 << 20),
    )(*args)


def scaled_std(kernel, gain):
    fan = kernel.shape[1]
    center = kernel - jnp.mean(kernel, axis=1, keepdims=True)
    spread = jnp.mean(jnp.square(center), axis=1, keepdims=True)
    return gain[:, None] * center * lax.rsqrt(fan * spread + eps_std)


def body(
    images, bucket, cotangent,
    narrow_kernel, narrow_gain, narrow_bias, first_kernel, first_gain, first_bias,
    second_kernel, second_gain, second_bias, widen_kernel, widen_gain, widen_bias,
    squeeze_kernel, squeeze_bias, excite_kernel, excite_bias, skip_gain,
):
    axes = ("batch", "row")
    devices = lax.axis_size(axes)
    fits = lax.axis_size("batch") == 8
    shape = images.shape
    kernels = [narrow_kernel, first_kernel, second_kernel, widen_kernel]
    maps = [squeeze_kernel, excite_kernel]
    gains = [narrow_gain, first_gain, second_gain, widen_gain]
    biases = [narrow_bias, first_bias, second_bias, widen_bias, squeeze_bias, excite_bias]
    if fits:
        rows = dict(enumerate(biases + [skip_gain])) | {8 + k: gain for k, gain in enumerate(gains)}
        vectors = sum(
            lax.pad(row.astype(F32)[None], jnp.zeros((), F32), ((k, 15 - k, 0), (0, 128 - row.shape[0], 0)))
            for k, row in rows.items())
        got = run_block(images, bucket, cotangent, kernels + maps, vectors, devices, True)
        got = own_results(got, [k.shape[0] for k in kernels + maps])
        output, input_grad = got[0], got[1]
        kernel_grads, gain_grads = got[2:8], [g.reshape(-1) for g in got[8:12]]
        bias_grads, skip_grad = [g.reshape(-1) for g in got[12:18]], got[18].reshape(1)
    else:
        gather = functools.partial(lax.all_gather, axis_name=axes, axis=0, tiled=True)
        scatter = functools.partial(lax.psum_scatter, axis_name=axes, scatter_dimension=0, tiled=True)
        floats = [(k.astype(F32), g.astype(F32)) for k, g in zip(kernels, gains)]
        of_row = functools.partial(lax.all_gather, axis_name="batch", axis=0, tiled=True)
        wholes = [gather(scaled_std(k, g).astype(BF)) for k, g in floats] + [of_row(m) for m in maps]
        width = shape[3]
        rows = [gather(bias).astype(F32) for bias in biases[:4]] + [of_row(bias).astype(F32) for bias in biases[4:]]
        rows += [skip_gain.astype(F32), jnp.zeros((1,), F32)]
        vectors = jnp.stack([jnp.pad(row, (0, width - row.shape[0])) for row in rows])
        got = run_block(images, bucket, cotangent, wholes, vectors, devices, False)
        output, input_grad = got[0], got[1]
        got = list(got)
        got[2:2 + GRAD_PIECES[0]] = [jnp.concatenate(got[2:2 + GRAD_PIECES[0]], axis=1)]
        totals = [scatter(g.astype(F32)) for g in got[2:6]]
        sums = got[7]
        to_row_owner = functools.partial(lax.psum_scatter, axis_name="batch", scatter_dimension=0, tiled=True)
        bias_grads = [(scatter if k < 4 else to_row_owner)(sums[k, :wholes[k].shape[0]]) for k in range(6)]
        skip_grad = lax.psum(sums[6, 0:1], axes)
        span, mid = maps[1].shape[0] * devices // 4, wholes[0].shape[0]
        values = of_row(got[6])
        cuts = [span, span + mid, span + mid + width, span + 2 * mid + width, 2 * span + 2 * mid + width]
        excited, hidden, pooled, third, pooled_grad, squeezed = jnp.split(values, cuts, axis=1)

        def own_rows(own, other, share):
            mine = lax.dynamic_slice_in_dim(own, lax.axis_index("batch") * share, share, axis=1)
            return dot(mine, other, TN)

        totals[3] += own_rows(pooled_grad, third, widen_kernel.shape[0])
        pulled = [jax.vjp(scaled_std, k, g)[1](t) for (k, g), t in zip(floats, totals)]
        kernel_grads, gain_grads = [p[0] for p in pulled], [p[1] for p in pulled]
        kernel_grads.append(own_rows(squeezed, pooled, squeeze_kernel.shape[0]))
        kernel_grads.append(own_rows(excited, hidden, excite_kernel.shape[0]))
    return (
        output.reshape(shape), input_grad.reshape(shape),
        kernel_grads[0], gain_grads[0], bias_grads[0],
        kernel_grads[1], gain_grads[1], bias_grads[1],
        kernel_grads[2], gain_grads[2], bias_grads[2],
        kernel_grads[3], gain_grads[3], bias_grads[3],
        kernel_grads[4], bias_grads[4], kernel_grads[5], bias_grads[5],
        skip_grad,
    )


def solution(mesh):
    maps, shared = P(None, "batch", "row", None), P(("batch", "row"))
    rows = P(("batch", "row"), None)
    weight = (rows, shared, shared)
    return jax.shard_map(
        body,
        mesh=mesh,
        in_specs=(maps, P(None, "batch"), maps, *weight * 4, rows, shared, rows, shared, P()),
        out_specs=(maps, maps, *weight * 4, rows, shared, rows, shared, P()),
        check_vma=False,
    )
```

time: 176 us -> 143 us (0.81)
  Pallas kernels: 155 us -> 140 us
  local copies, waits for them, and re-layouts: 14.3 us -> 0 us
  other arithmetic: 4.02 us -> 1.41 us
    pallas_call x1 -> x2, Pallas kernels: 155 us -> 140 us  [the longest x1 135 us: run_block(): pl.pallas_call(kernel, out_shape=outs, in_specs=specs, out_specs=[anywher...]
    unnamed x52 -> x0, local copies, waits for them, and re-layouts: 13.1 us -> none
    another operation x6 -> x0, other arithmetic: 4.02 us -> none  [body(): vectors = jnp.stack([padded(row) for row in rows])]
where the time goes in v2:
time: 143 us
  Pallas kernels  140 us (98%)
  between operations  1.48 us (1%)
    pallas_call x1, Pallas kernels, run_block(): pl.pallas_call(kernel, out_shape=outs, in_specs=specs, out_specs=[anywher...  135 us
    pallas_call x1, Pallas kernels, own_results(): pl.pallas_call(hand_over, grid=(steps,), out_shape=results, in_specs=spec...  4.84 us

profile of v2, /device:TPU:0, one launch (start us, length us, event | category | flops | bytes accessed | tf_op | source)
XLA Modules:
  0.0 143.1 jit_solution(3302292274722328644)
XLA Ops:
  1.3 1.4 convert_add_fusion.refs_9_
  2.7 135.4 %shard_map.339 = (bf16[512,1536]{1,0:T(8,128)(2,1)}, bf16[512,1536]{1,0:T(8,128)(2,1)}, f32[24,1536]{1,0:T(8,128)}, f32[24,1152]{1,0:T(8,128)}, f32[24,1152]{1,0...) custom-call(s32[2,8]{1,0:T(2,128)} %refs_0_.1, ...), custom_call_target="tpu_custom_call" | custom-call | tf_op jit(solution)/shard_map/pallas_call | solution.py:1239
  138.1 4.8 %shard_map.340 = (bf16[512,1536]{1,0:T(8,128)(2,1)}, bf16[512,1536]{1,0:T(8,128)(2,1)}, f32[24,1536]{1,0:T(8,128)}, f32[24,1152]{1,0:T(8,128)}, f32[24,1152]{1,0...) custom-call(bf16[512,1536]{1,0:T(8,128)(2,1)} %get-tuple-element.47., ...), custom_call_target="tpu_custom_call" | custom-call | tf_op jit(solution)/shard_map/pallas_call | solution.py:1105
